TPU v7x, 32 devices: a whole 2x2x4 slice. The times are simulated.
32 devices in a mesh: blk: 8 (over y, x, core), narrow: 4 (over z).
Axes of the slice: x: 2, y: 2, z: 4, core: 2. Of those that a mesh axis runs over, the one named last changes fastest.
Arguments:
- codes: bfloat16 [6144, 12288], P(('blk', 'narrow')), may hold values from -6 to 6
- signals: bfloat16 [6144, 192], P(('blk', 'narrow')), may hold values from -6 to 6
- dictionary: bfloat16 [12288, 192], P('blk'), may hold values from -0.0546875 to 0.0546875
Outputs:
- new_codes: bfloat16 [6144, 12288], P(('blk', 'narrow'))
- dict_grad: float32 [12288, 192], P(('blk', 'narrow'))
All inputs are finite; a program needn't handle non-finite values.
Results may differ from a plain program's by a relative error of at most 0.0095.
Values may be sent and summed in bfloat16 or wider, within the bound.
A program may use at most 64 MiB of HBM per device.

v0:
```python
import jax
import jax.numpy as jnp
from jax import lax
from jax.sharding import PartitionSpec as P


def shrink(values):
    return jnp.sign(values) * jnp.maximum(jnp.abs(values) - 0.5, 0.0)


def body(codes, signals, dictionary):
    row_count = codes.shape[0]
    blk_size = lax.axis_size("blk")
    narrow_size = lax.axis_size("narrow")
    signal_float = signals.astype(jnp.float32)
    columns = codes
    estimate = jnp.dot(
        columns,
        lax.all_gather(dictionary, "blk", axis=0, tiled=True),
        preferred_element_type=jnp.float32,
    )
    misfit = (estimate - signal_float).astype(jnp.bfloat16)
    atoms_part = lax.all_gather(dictionary, "blk", axis=0, tiled=True)
    columns = codes
    correlation = lax.dot_general(
        misfit, atoms_part, (((1,), (1,)), ((), ())), preferred_element_type=jnp.float32
    )
    fresh_cols = shrink(columns.astype(jnp.float32) - 4.0 * correlation).astype(jnp.bfloat16)
    second = jnp.dot(fresh_cols, atoms_part, preferred_element_type=jnp.float32)
    misfit_two = (second - signal_float).astype(jnp.bfloat16)
    grad_scale = float(row_count * blk_size * narrow_size) ** (-0.5)
    columns = fresh_cols
    product = lax.dot_general(
        columns, misfit_two, (((0,), (0,)), ((), ())), preferred_element_type=jnp.float32
    )
    partial_grad = lax.psum_scatter(
        (product * grad_scale).astype(jnp.bfloat16), "blk", scatter_dimension=0, tiled=True
    )
    dict_grad = lax.psum_scatter(partial_grad, "narrow", scatter_dimension=0, tiled=True).astype(
        jnp.float32
    )
    return (fresh_cols, dict_grad)


def solution(mesh):
    placed = (P(("blk", "narrow"), None), P(("blk", "narrow"), None), P("blk", None))
    return jax.shard_map(
        body,
        mesh=mesh,
        in_specs=placed,
        out_specs=(P(("blk", "narrow"), None), P(("blk", "narrow"), None)),
        check_vma=False,
    )
```

profile of v0, /device:TPU:0, one launch (start us, length us, event | category | flops | bytes accessed | tf_op | source)
XLA Modules:
  0.0 164.6 jit_solution(11495334058509658674)
XLA Ops:
  7.2 0.0 all-gather.2.cloned.1.call-start
  7.2 0.7 all-gather.2.cloned.1.call-update
  7.9 0.0 copy-start.1
  7.9 0.0 reduce-scatter.5.cloned.1.call-start
  8.0 43.6 %all-gather.2.cloned.1.call-done = bf16[12288,192]{0,1:T(8,128)(2,1)} async-done(((bf16[1536,192]{0,1:T(8,128)(2,1)}), bf16[12288,192]{0,1:T(8,128)(2,1)}) %all-gather.2.cloned.1.call-update) | async-done | bytes 4718608 | tf_op jit(solution)/shard_map/all_gather | solution.py:19
  51.6 16.0 %multiply_convert_fusion = bf16[192,12288]{1,0:T(8,128)(2,1)} fusion(bf16[12288,192]{0,1:T(8,128)(2,1)} %all-gather.2.cloned.1.call-done, bf16[192,12288]{1,0:T(8,128)(2,1)} %param.3, bf16[192,192]{1,0:T(8,128)(2,1)} %param.4), kind=kOutput, calls=%fused_computation.4 | convolution fusion | flops 1833283584 | bytes 14229504 | tf_op jit(solution)/shard_map/dot_general | solution.py:25
  67.6 0.0 copy-done.1
  67.6 0.0 copy-start
  67.6 5.3 %fusion.3 = bf16[192,192]{1,0:T(8,128)(2,1)S(1)} fusion(bf16[192,12288]{1,0:T(8,128)(2,1)} %multiply_convert_fusion, bf16[12288,192]{0,1:T(8,128)(2,1)} %all-gather.2.cloned.1.call-done, bf16[192,192]{1,0:T(8,128)(2,1)S(1)} %copy-done.1), kind=kOutput, calls=%fused_computation.8 | convolution fusion | flops 906080256 | bytes 9584640 | tf_op jit(solution)/shard_map/dot_general | solution.py:29
  72.9 0.0 copy-done
  72.9 3.6 %fusion.1 = bf16[12288,192]{0,1:T(8,128)(2,1)} fusion(bf16[192,12288]{1,0:T(8,128)(2,1)S(1)} %copy-done, bf16[192,192]{1,0:T(8,128)(2,1)S(1)} %fusion.3), kind=kOutput, calls=%fused_computation.3 | convolution fusion | flops 910688256 | bytes 9510912 | tf_op jit(solution)/shard_map/dot_general | solution.py:33
  76.5 0.0 reduce-scatter.5.cloned.1.call-update
  76.5 0.0 reduce-scatter.7.cloned.1.call-start
  76.6 54.0 %reduce-scatter.5.cloned.1.call-done = bf16[1536,192]{0,1:T(8,128)(2,1)} async-done(((bf16[12288,192]{0,1:T(8,128)(2,1)}), bf16[1536,192]{0,1:T(8,128)(2,1)}) %reduce-scatter.5.cloned.1.call-update) | async-done | bytes 589840 | tf_op jit(solution)/shard_map/reduce_scatter | solution.py:36
  130.6 2.2 %copy.5 = bf16[1536,192]{1,0:T(8,128)(2,1)} copy(bf16[1536,192]{0,1:T(8,128)(2,1)} %reduce-scatter.5.cloned.1.call-done) | data formatting | bytes 1179648
  132.8 0.0 reduce-scatter.7.cloned.1.call-update
  132.8 23.5 %reduce-scatter.7.cloned.1.call-done = bf16[384,192]{1,0:T(8,128)(2,1)} async-done(((bf16[1536,192]{1,0:T(8,128)(2,1)}), bf16[384,192]{1,0:T(8,128)(2,1)}) %reduce-scatter.7.cloned.1.call-update) | async-done | bytes 147472
  156.3 1.1 copy.6
  157.4 0.7 convert_element_type.27
Async XLA Ops:
  7.2 44.4 %all-gather.2.cloned.1.call-start = ((), (), s32[]{:S(2)}) async-start(), calls=%async_computation.2 | async-start | bytes 5308416 | tf_op jit(solution)/shard_map/all_gather | solution.py:19
  7.9 59.7 %copy-start.1 = (bf16[192,192]{1,0:T(8,128)(2,1)S(1)}, bf16[192,192]{1,0:T(8,128)(2,1)}, u32[]{:S(2)}) copy-start(bf16[192,192]{1,0:T(8,128)(2,1)} %param.4) | copy-start | bytes 221188
  7.9 122.7 %reduce-scatter.5.cloned.1.call-start = ((), (), s32[]{:S(2)}) async-start(), calls=%async_computation.3 | async-start | bytes 5308416 | tf_op jit(solution)/shard_map/reduce_scatter | solution.py:36
  67.6 5.3 %copy-start = (bf16[192,12288]{1,0:T(8,128)(2,1)S(1)}, bf16[192,12288]{1,0:T(8,128)(2,1)}, u32[]{:S(2)}) copy-start(bf16[192,12288]{1,0:T(8,128)(2,1)} %multiply_convert_fusion) | copy-start | bytes 14155780
  76.5 79.8 %reduce-scatter.7.cloned.1.call-start = ((), (), s32[]{:S(2)}) async-start(), calls=%async_computation.4 | async-start | bytes 983040
Sparse Core Ops, SparseCore 0:
  9.9 41.6 all-gather.1
  76.7 53.8 reduce-scatter.4
  133.0 23.2 reduce-scatter.6
where the time goes:
time: 165 us
  waiting for transfers between devices  122 us (74%)
  matrix products  24.9 us (15%)
  between operations  13.8 us (8%)
  local copies, waits for them, and re-layouts  3.3 us (2%)
    reduce_scatter x1, waiting for transfers between devices, body(): lax.psum_scatter((product * grad_scale).astype(jnp.bfloat16), 'blk', scat...  54 us
    all_gather x1, waiting for transfers between devices, body(): lax.all_gather(dictionary, 'blk', axis=0, tiled=True)  43.6 us
    unnamed x4, waiting for transfers between devices  24.2 us
    dot_general x1, matrix products, body(): lax.dot_general(misfit, atoms_part, (((1,), (1,)), ((), ())), preferred_e...  16 us
    dot_general x1, matrix products, body(): second = jnp.dot(fresh_cols, atoms_part, preferred_element_type=jnp.float32)  5.3 us
    dot_general x1, matrix products, body(): lax.dot_general(columns, misfit_two, (((0,), (0,)), ((), ())), preferred_...  3.61 us
    unnamed x6, local copies, waits for them, and re-layouts  3.3 us
  transfers between devices with their start and end apart: 3, of which 3 were waited for; matrix products, arithmetic and copies ran while one was open for 0% of the time, Pallas kernels for 0%

commit v1 on v0

v1 whole, which is shorter than its diff:
```python
import functools

import jax
import jax.numpy as jnp
from jax import lax
from jax.experimental import pallas as pl
from jax.experimental.pallas import tpu as pltpu
from jax.sharding import PartitionSpec as P

MESH = pl.DeviceIdType.MESH
VMEM = pltpu.VMEM
DMA = pltpu.SemaphoreType.DMA
HALVES = 2
CORES = 2


def flip(chip, distance):
    bit = 1
    while bit <= distance:
        if distance & bit:
            chip = chip + bit * (1 - 2 * ((chip // bit) % 2))
        bit *= 2
    return chip


def low(d):
    return d & -d


def high(d):
    return 1 << (d.bit_length() - 1)


def ones(d):
    return bin(d).count("1")


def bits_of(chips):
    return [1 << i for i in range(chips.bit_length() - 1)]


def toward(d, half):
    return low(d) if half == 0 else high(d)


def children(d, half, bits):
    return [b for b in bits if d == 0 or (b < low(d) if half == 0 else b > high(d))]


def pieces_of(chips):
    return [(d, h) for d in range(chips) for h in range(HALVES)]


def nt_dot(a, b):
    return lax.dot_general(a, b, (((1,), (1,)), ((), ())), preferred_element_type=jnp.float32)


def gather_kernel(
    chips, codes, signals, atoms, full, misfit, held, total,
    load_sem, atom_sem, net_send, net_recv, core_send, core_recv,
):
    bits = bits_of(chips)
    me = lax.axis_index("blk")
    chip, core = me // CORES, me % CORES
    other = CORES * chip + 1 - core
    width = full.shape[2]

    def owner(d, c):
        return CORES * flip(chip, d) + c

    order = sorted(
        pieces_of(chips),
        key=lambda p: (ones(p[0]), -len(children(p[0], p[1], bits)), p[0]),
    )
    uses = [(d, h, c) for d, h in order for c in range(CORES)]

    def atom_copy(h):
        return pltpu.make_async_copy(
            atoms.at[:, pl.ds(h * width, width)], full.at[me * HALVES + h], atom_sem.at[h]
        )

    def block(d, h, c):
        return owner(d, core if c == 0 else 1 - core) * HALVES + h

    def load(slot):
        d, h, c = uses[slot]
        start = pl.multiple_of(block(d, h, c) * width, width)
        return pltpu.make_async_copy(
            codes.at[:, pl.ds(start, width)], held.at[slot], load_sem.at[slot]
        )

    for h in range(HALVES):
        atom_copy(h).start()
    partners = [other] + [CORES * flip(chip, b) + core for b in bits]
    barrier = pltpu.get_barrier_semaphore()
    for partner in partners:
        pl.semaphore_signal(barrier, inc=1, device_id={"blk": partner}, device_id_type=MESH)
    for slot in range(len(uses)):
        load(slot).start()

    sends = []

    def net(d, h, b):
        place = full.at[block(d, h, 0)]
        copy = pltpu.make_async_remote_copy(
            place, place, net_send.at[len(sends)], net_recv.at[(d ^ b) * HALVES + h],
            device_id={"blk": CORES * flip(chip, b) + core}, device_id_type=MESH,
        )
        copy.start()
        sends.append(copy)

    def across(d, h, c):
        place = full.at[block(d, h, c)]
        index = d * HALVES + h
        return pltpu.make_async_remote_copy(
            place, place, core_send.at[index], core_recv.at[index],
            device_id={"blk": other}, device_id_type=MESH,
        )

    def arrived(d, h):
        place = full.at[block(d, h, 0)]
        pltpu.make_async_remote_copy(
            place, place, net_send.at[0], net_recv.at[d * HALVES + h],
            device_id={"blk": other}, device_id_type=MESH,
        ).wait_recv()

    def use(d, h, c):
        slot = uses.index((d, h, c))
        load(slot).wait()
        total[...] += nt_dot(held[slot], full[block(d, h, c)])

    for h in range(HALVES):
        atom_copy(h).wait()
    pl.semaphore_wait(barrier, len(partners))
    for step in range(HALVES):
        for i, b in enumerate(bits):
            h = 1 - step if i == 0 else step
            net(0, h, b)
        across(0, step, 0).start()
    total[...] = jnp.zeros_like(total)
    waiting = []
    for d, h in order:
        if d:
            arrived(d, h)
            for b in children(d, h, bits):
                net(d, h, b)
            across(d, h, 0).start()
        use(d, h, 0)
        waiting.append((d, h))
        if len(waiting) > 1:
            e, k = waiting.pop(0)
            across(e, k, 1).wait_recv()
            use(e, k, 1)
    for e, k in waiting:
        across(e, k, 1).wait_recv()
        use(e, k, 1)
    rounded = (total[...] - signals[...].astype(jnp.float32)).astype(jnp.bfloat16)
    misfit[...] = (rounded.astype(jnp.float32) * -4.0).astype(jnp.bfloat16)
    for copy in sends:
        copy.wait_send()
    for d, h in order:
        across(d, h, 0).wait_send()


def update_kernel(codes, signals, full, misfit, fresh, misfit_two, total):
    step = pl.program_id(0)

    @pl.when(step == 0)
    def _():
        total[...] = jnp.zeros_like(total)

    change = jnp.dot(misfit[...], full[0], preferred_element_type=jnp.float32)
    moved = codes[...].astype(jnp.float32) + change
    shrunk = (moved - jnp.clip(moved, -0.5, 0.5)).astype(jnp.bfloat16)
    fresh[...] = shrunk
    total[...] += nt_dot(shrunk, full[0])

    @pl.when(step == pl.num_programs(0) - 1)
    def _():
        left = total[...] - signals[...].astype(jnp.float32)
        misfit_two[...] = left.T.astype(jnp.bfloat16)


def gradient_kernel(
    chips, line, scale, fresh, misfit, grad,
    held, core_out, core_in, net_out, net_in, own, z_out, z_in,
    load_sem, core_send, core_recv, net_send, net_recv, z_send, z_recv,
):
    bits = bits_of(chips)
    me = lax.axis_index("blk")
    z = lax.axis_index("narrow")
    chip, core = me // CORES, me % CORES
    other = CORES * chip + 1 - core
    width = held.shape[2]
    part = grad.shape[1]

    order = sorted(
        pieces_of(chips),
        key=lambda p: (-ones(p[0]), len(children(p[0], p[1], bits)), p[0]),
    )
    uses = [(d, h, c) for d, h in order for c in (1, 0)]
    entries = [(d, h, b) for d, h in order for b in children(d, h, bits)]

    def load(slot):
        d, h, c = uses[slot]
        owner = CORES * flip(chip, d) + (core if c == 0 else 1 - core)
        start = pl.multiple_of((owner * HALVES + h) * width, width)
        return pltpu.make_async_copy(
            fresh.at[:, pl.ds(start, width)], held.at[slot], load_sem.at[slot]
        )

    for slot in range(len(uses)):
        load(slot).start()
    barrier = pltpu.get_barrier_semaphore()
    partners = [other] + [CORES * flip(chip, b) + core for b in bits]
    for partner in partners:
        pl.semaphore_signal(barrier, inc=1, device_id={"blk": partner}, device_id_type=MESH)
    beside = [(z + 1) % line, (z + line - 1) % line] if line > 1 else []
    for partner in beside:
        pl.semaphore_signal(barrier, inc=1, device_id={"narrow": partner}, device_id_type=MESH)

    def term(d, h, c):
        slot = uses.index((d, h, c))
        load(slot).wait()
        return jnp.dot(misfit[...], held[slot], preferred_element_type=jnp.float32)

    def across(i):
        return pltpu.make_async_remote_copy(
            core_out.at[i], core_in.at[i], core_send.at[i], core_recv.at[i],
            device_id={"blk": other}, device_id_type=MESH,
        )

    def net(i, slot, b):
        return pltpu.make_async_remote_copy(
            net_out.at[i], net_in.at[slot], net_send.at[i], net_recv.at[slot],
            device_id={"blk": CORES * flip(chip, b) + core}, device_id_type=MESH,
        )

    def hand_over(i):
        d, h = order[i]
        core_out[i] = term(d, h, 1).astype(jnp.bfloat16)
        if i == 0:
            pl.semaphore_wait(barrier, len(partners) + len(beside))
        across(i).start()

    ahead = min(2, len(order))
    for i in range(ahead):
        hand_over(i)
    sends = []
    for i, (d, h) in enumerate(order):
        if i + ahead < len(order):
            hand_over(i + ahead)
        value = term(d, h, 0)
        across(i).wait_recv()
        value += core_in[i].astype(jnp.float32)
        for b in children(d, h, bits):
            slot = entries.index((d, h, b))
            net(0, slot, b).wait_recv()
            value += net_in[slot].astype(jnp.float32)
        if d:
            b = toward(d, h)
            net_out[i] = value.astype(jnp.bfloat16)
            copy = net(i, entries.index((d ^ b, h, b)), b)
            copy.start()
            sends.append(copy)
        else:
            for j in range(width // part):
                own[h * (width // part) + j] = value[:, j * part:(j + 1) * part]

    def z_copy(side, t):
        return pltpu.make_async_remote_copy(
            z_out.at[side, t], z_in.at[side, t - 1],
            z_send.at[side, t], z_recv.at[side, t - 1],
            device_id={"narrow": z + 1 if side == 0 else z - 1}, device_id_type=MESH,
        )

    def z_arrived(side, t):
        pltpu.make_async_remote_copy(
            z_out.at[side, 0], z_in.at[side, t], z_send.at[side, 0], z_recv.at[side, t],
            device_id={"narrow": z - 1 if side == 0 else z + 1}, device_id_type=MESH,
        ).wait_recv()

    def has_behind(side):
        return z >= 1 if side == 0 else z <= line - 2

    def in_line(side, t):
        return z + t < line if side == 0 else z - t >= 0

    for t in range(line - 1, 0, -1):
        for side in range(2):
            @pl.when(in_line(side, t))
            def _():
                mine = own[z + t if side == 0 else z - t]

                @pl.when(has_behind(side))
                def _():
                    z_arrived(side, t)
                    z_out[side, t] = (mine + z_in[side, t].astype(jnp.float32)).astype(jnp.bfloat16)

                @pl.when(jnp.logical_not(has_behind(side)))
                def _():
                    z_out[side, t] = mine.astype(jnp.bfloat16)

                z_copy(side, t).start()

    grad[...] = own[z]
    if line > 1:
        for side in range(2):
            @pl.when(has_behind(side))
            def _():
                z_arrived(side, 0)
                grad[...] += z_in[side, 0].astype(jnp.float32)
    grad[...] = grad[...] * scale

    for t in range(line - 1, 0, -1):
        for side in range(2):
            @pl.when(in_line(side, t))
            def _():
                z_copy(side, t).wait_send()
    for copy in sends:
        copy.wait_send()
    for i in range(len(order)):
        across(i).wait_send()


def body(blk, line, codes, signals, dictionary):
    rows, count = codes.shape
    atoms, features = dictionary.shape
    chips = blk // CORES
    width = atoms // HALVES
    blocks = blk * HALVES
    pieces = chips * HALVES
    links = len(bits_of(chips))
    part = atoms // line
    bf16, f32 = jnp.bfloat16, jnp.float32
    any_spec = pl.BlockSpec(memory_space=pl.ANY)
    vmem_spec = pl.BlockSpec(memory_space=VMEM)
    flops = 2 * rows * count * features
    size = 2 * rows * count

    full, misfit = pl.pallas_call(
        functools.partial(gather_kernel, chips),
        out_shape=(
            jax.ShapeDtypeStruct((blocks, features, width), bf16),
            jax.ShapeDtypeStruct((rows, features), bf16),
        ),
        in_specs=[any_spec, vmem_spec, any_spec],
        out_specs=(vmem_spec, vmem_spec),
        scratch_shapes=[
            VMEM((blocks, rows, width), bf16),
            VMEM((rows, features), f32),
            DMA((blocks,)), DMA((HALVES,)),
            DMA((HALVES * max(chips - 1, 1),)), DMA((pieces,)),
            DMA((pieces,)), DMA((pieces,)),
        ],
        compiler_params=pltpu.CompilerParams(
            collective_id=0, has_side_effects=True, vmem_limit_bytes=32 * 2**20
        ),
        cost_estimate=pl.CostEstimate(flops=flops, bytes_accessed=2 * size, transcendentals=0),
        name="gather_atoms",
    )(codes, signals, dictionary.T)

    fresh, misfit_two = pl.pallas_call(
        update_kernel,
        grid=(blocks,),
        out_shape=(
            jax.ShapeDtypeStruct((rows, count), bf16),
            jax.ShapeDtypeStruct((features, rows), bf16),
        ),
        in_specs=[
            pl.BlockSpec((rows, width), lambda i: (0, i)),
            pl.BlockSpec((rows, features), lambda i: (0, 0)),
            pl.BlockSpec((1, features, width), lambda i: (i, 0, 0)),
            pl.BlockSpec((rows, features), lambda i: (0, 0)),
        ],
        out_specs=(
            pl.BlockSpec((rows, width), lambda i: (0, i)),
            pl.BlockSpec((features, rows), lambda i: (0, 0)),
        ),
        scratch_shapes=[VMEM((rows, features), f32)],
        compiler_params=pltpu.CompilerParams(vmem_limit_bytes=24 * 2**20),
        cost_estimate=pl.CostEstimate(flops=2 * flops, bytes_accessed=3 * size, transcendentals=0),
        name="update_codes",
    )(codes, signals, full, misfit)

    grad = pl.pallas_call(
        functools.partial(gradient_kernel, chips, line, float(rows * blk * line) ** -0.5),
        out_shape=jax.ShapeDtypeStruct((features, part), f32),
        in_specs=[any_spec, vmem_spec],
        out_specs=vmem_spec,
        scratch_shapes=[
            VMEM((blocks, rows, width), bf16),
            VMEM((pieces, features, width), bf16),
            VMEM((pieces, features, width), bf16),
            VMEM((pieces, features, width), bf16),
            VMEM((max(HALVES * (chips - 1), 1), features, width), bf16),
            VMEM((line, features, part), f32),
            VMEM((2, line, features, part), bf16),
            VMEM((2, line, features, part), bf16),
            DMA((blocks,)), DMA((pieces,)), DMA((pieces,)), DMA((pieces,)),
            DMA((max(HALVES * (chips - 1), 1),)), DMA((2, line)), DMA((2, line)),
        ],
        compiler_params=pltpu.CompilerParams(
            collective_id=1, has_side_effects=True, vmem_limit_bytes=40 * 2**20
        ),
        cost_estimate=pl.CostEstimate(flops=flops, bytes_accessed=2 * size, transcendentals=0),
        name="dictionary_gradient",
    )(fresh, misfit_two)
    return fresh, grad.T


def solution(mesh):
    placed = (P(("blk", "narrow"), None), P(("blk", "narrow"), None), P("blk", None))
    return jax.shard_map(
        functools.partial(body, mesh.shape["blk"], mesh.shape["narrow"]),
        mesh=mesh,
        in_specs=placed,
        out_specs=(P(("blk", "narrow"), None), P(("blk", "narrow"), None)),
        check_vma=False,
    )
```

time: 165 us -> 85.8 us (0.52)
  waiting for transfers between devices: 122 us -> 0 us
  Pallas kernels: 0 us -> 77.3 us
  matrix products: 24.9 us -> 0 us
  between operations: 13.8 us -> 0.67 us
  local copies, waits for them, and re-layouts: 3.3 us -> 7.34 us
    pallas_call x0 -> x3, Pallas kernels: none -> 77.3 us  [the longest x1 41.5 us: body(): pl.pallas_call(functools.partial(gradient_kernel, chips, line, float(rows...]
    reduce_scatter x1 -> x0, waiting for transfers between devices: 54 us -> none  [body(): lax.psum_scatter((product * grad_scale).astype(jnp.bfloat16), 'blk', scat...]
    all_gather x1 -> x0, waiting for transfers between devices: 43.6 us -> none  [body(): lax.all_gather(dictionary, 'blk', axis=0, tiled=True)]
    dot_general x3 -> x0, matrix products: 24.9 us -> none  [the longest x1 16 us: body(): lax.dot_general(misfit, atoms_part, (((1,), (1,)), ((), ())), preferred_e...]
    unnamed x4 -> x0, waiting for transfers between devices: 24.2 us -> none
    unnamed x6 -> x11, local copies, waits for them, and re-layouts: 3.3 us -> 7.34 us
  transfers between devices with their start and end apart: 3 -> 0, of which waited for: 3 -> 0; matrix products, arithmetic and copies ran while one was open for 0% -> 0% of each run, Pallas kernels for 0% -> 0%
where the time goes in v1:
time: 85.8 us; the launch traced here: 85.3 us
  Pallas kernels  77.3 us (90%)
  local copies, waits for them, and re-layouts  7.34 us (9%)
    pallas_call x1, Pallas kernels, body(): pl.pallas_call(functools.partial(gradient_kernel, chips, line, float(rows...  41.5 us
    pallas_call x1, Pallas kernels, body(): pl.pallas_call(functools.partial(gather_kernel, chips), out_shape=(jax.Sh...  26.2 us
    pallas_call x1, Pallas kernels, body(): pl.pallas_call(update_kernel, grid=(blocks,), out_shape=(jax.ShapeDtypeSt...  9.67 us
    unnamed x11, local copies, waits for them, and re-layouts  7.34 us

profile of v1, /device:TPU:0, one launch (start us, length us, event | category | flops | bytes accessed | tf_op | source)
XLA Modules:
  0.0 85.3 jit_solution(4702757719401574500)
XLA Ops:
  0.6 0.0 copy-start
  0.6 2.3 %copy-done = bf16[192,12288]{1,0:T(8,128)(2,1)S(1)} copy-done((bf16[192,12288]{1,0:T(8,128)(2,1)S(1)}, bf16[192,12288]{1,0:T(8,128)(2,1)}, u32[]{:S(2)}) %copy-start) | copy-done | bytes 4718616
  3.0 0.0 copy-start.3
  3.0 1.1 %copy-done.3 = bf16[1536,192]{0,1:T(8,128)(2,1)S(1)} copy-done((bf16[1536,192]{0,1:T(8,128)(2,1)S(1)}, bf16[1536,192]{0,1:T(8,128)(2,1)}, u32[]{:S(2)}) %copy-start.3) | copy-done | bytes 589848
  4.0 0.0 copy-start.4
  4.0 0.9 %copy-done.4 = bf16[192,192]{1,0:T(8,128)(2,1)S(1)} copy-done((bf16[192,192]{1,0:T(8,128)(2,1)S(1)}, bf16[192,192]{1,0:T(8,128)(2,1)}, u32[]{:S(2)}) %copy-start.4) | copy-done | bytes 73752
  4.9 0.0 copy-start.1
  4.9 26.2 %gather_atoms.1 = (bf16[16,192,768]{2,1,0:T(8,128)(2,1)S(1)}, bf16[192,192]{1,0:T(8,128)(2,1)S(1)}) custom-call(bf16[192,12288]{1,0:T(8,128)(2,1)S(1)} %copy-done, bf16[192,192]{1,0:T(8,128)(2,1)S(1)} %copy-done.4, bf16[192,1536]{1,0:T(8,128)(2,1)S(1)} %bitcast.3), custom_call_target="tpu_custom_call" | custom-call | flops 905969664 | bytes 9437184 | tf_op jit(solution)/shard_map/gather_atoms/pallas_call | solution.py:341
  31.1 0.0 copy-done.1
  31.1 9.7 %update_codes.1 = (bf16[192,12288]{1,0:T(8,128)(2,1)}, bf16[192,192]{1,0:T(8,128)(2,1)S(1)}) custom-call(bf16[192,12288]{1,0:T(8,128)(2,1)S(1)} %copy-done.1, bf16[192,192]{1,0:T(8,128)(2,1)S(1)} %copy-done.4, bf16[16,192,768]{2,1,0:T(8,128)(2,1)S(1)} %get-tuple-element.6.full, bf16[192,192]{1,0:T(8,128)(2,1)S(1)} %get-tuple-element.7.misfit), custom_call_target="tpu_custom_call" | custom-call | flops 1811939328 | bytes 14155776 | tf_op jit(solution)/shard_map/update_codes/pallas_call | solution.py:363
  40.8 0.0 copy-start.2
  40.8 2.3 %copy-done.2 = bf16[192,12288]{1,0:T(8,128)(2,1)S(1)} copy-done((bf16[192,12288]{1,0:T(8,128)(2,1)S(1)}, bf16[192,12288]{1,0:T(8,128)(2,1)}, u32[]{:S(2)}) %copy-start.2) | copy-done | bytes 4718616
  43.1 41.5 %dictionary_gradient.1 = f32[192,384]{1,0:T(8,128)S(1)} custom-call(bf16[192,12288]{1,0:T(8,128)(2,1)S(1)} %copy-done.2, bf16[192,192]{1,0:T(8,128)(2,1)S(1)} %get-tuple-element.9.misfit), custom_call_target="tpu_custom_call" | custom-call | flops 905969664 | bytes 9437184 | tf_op jit(solution)/shard_map/dictionary_gradient/pallas_call | solution.py:386
  84.6 0.7 copy.6
Async XLA Ops:
  0.6 2.3 %copy-start = (bf16[192,12288]{1,0:T(8,128)(2,1)S(1)}, bf16[192,12288]{1,0:T(8,128)(2,1)}, u32[]{:S(2)}) copy-start(bf16[192,12288]{1,0:T(8,128)(2,1)} %codes.3) | copy-start | bytes 14155780
  3.0 1.1 %copy-start.3 = (bf16[1536,192]{0,1:T(8,128)(2,1)S(1)}, bf16[1536,192]{0,1:T(8,128)(2,1)}, u32[]{:S(2)}) copy-start(bf16[1536,192]{0,1:T(8,128)(2,1)} %param.5) | copy-start | bytes 1769476
  4.0 0.9 %copy-start.4 = (bf16[192,192]{1,0:T(8,128)(2,1)S(1)}, bf16[192,192]{1,0:T(8,128)(2,1)}, u32[]{:S(2)}) copy-start(bf16[192,192]{1,0:T(8,128)(2,1)} %signals.3) | copy-start | bytes 221188
  4.9 26.2 %copy-start.1 = (bf16[192,12288]{1,0:T(8,128)(2,1)S(1)}, bf16[192,12288]{1,0:T(8,128)(2,1)}, u32[]{:S(2)}) copy-start(bf16[192,12288]{1,0:T(8,128)(2,1)} %codes.3) | copy-start | bytes 14155780
  40.8 2.3 %copy-start.2 = (bf16[192,12288]{1,0:T(8,128)(2,1)S(1)}, bf16[192,12288]{1,0:T(8,128)(2,1)}, u32[]{:S(2)}) copy-start(bf16[192,12288]{1,0:T(8,128)(2,1)} %get-tuple-element.12.fresh) | copy-start | bytes 14155780

commit v2 on v1

--- a/solution.py
+++ b/solution.py
@@ -56,8 +56,8 @@
 
 
 def gather_kernel(
-    chips, codes, signals, atoms, full, misfit, held, total,
-    load_sem, atom_sem, net_send, net_recv, core_send, core_recv,
+    chips, codes, signals, atoms, full, misfit, held, target, total,
+    load_sem, target_sem, atom_sem, net_send, net_recv, core_send, core_recv,
 ):
     bits = bits_of(chips)
     me = lax.axis_index("blk")
@@ -97,6 +97,9 @@
         pl.semaphore_signal(barrier, inc=1, device_id={"blk": partner}, device_id_type=MESH)
     for slot in range(len(uses)):
         load(slot).start()
+
+    target_copy = pltpu.make_async_copy(signals, target, target_sem)
+    target_copy.start()
 
     sends = []
 
@@ -154,7 +157,8 @@
     for e, k in waiting:
         across(e, k, 1).wait_recv()
         use(e, k, 1)
-    rounded = (total[...] - signals[...].astype(jnp.float32)).astype(jnp.bfloat16)
+    target_copy.wait()
+    rounded = (total[...] - target[...].astype(jnp.float32)).astype(jnp.bfloat16)
     misfit[...] = (rounded.astype(jnp.float32) * -4.0).astype(jnp.bfloat16)
     for copy in sends:
         copy.wait_send()
@@ -162,23 +166,34 @@
         across(d, h, 0).wait_send()
 
 
-def update_kernel(codes, signals, full, misfit, fresh, misfit_two, total):
-    step = pl.program_id(0)
-
-    @pl.when(step == 0)
-    def _():
-        total[...] = jnp.zeros_like(total)
-
-    change = jnp.dot(misfit[...], full[0], preferred_element_type=jnp.float32)
-    moved = codes[...].astype(jnp.float32) + change
-    shrunk = (moved - jnp.clip(moved, -0.5, 0.5)).astype(jnp.bfloat16)
-    fresh[...] = shrunk
-    total[...] += nt_dot(shrunk, full[0])
-
-    @pl.when(step == pl.num_programs(0) - 1)
-    def _():
-        left = total[...] - signals[...].astype(jnp.float32)
-        misfit_two[...] = left.T.astype(jnp.bfloat16)
+def update_kernel(together, codes, signals, full, misfit, fresh, misfit_two, made, total, store_sem):
+    blocks, _, width = full.shape
+
+    def store(i):
+        start = pl.multiple_of(i * width, width)
+        return pltpu.make_async_copy(
+            made.at[i], fresh.at[:, pl.ds(start, width)], store_sem.at[i]
+        )
+
+    total[...] = jnp.zeros_like(total)
+
+    @pl.loop(0, blocks // together)
+    def _(step):
+        for j in range(together):
+            i = step * together + j
+            start = pl.multiple_of(i * width, width)
+            change = jnp.dot(misfit[...], full[i], preferred_element_type=jnp.float32)
+            moved = codes[:, pl.ds(start, width)].astype(jnp.float32) + change
+            made[i] = (moved - jnp.clip(moved, -0.5, 0.5)).astype(jnp.bfloat16)
+            store(i).start()
+        for j in range(together):
+            i = step * together + j
+            total[...] += nt_dot(made[i], full[i])
+
+    left = total[...] - signals[...].astype(jnp.float32)
+    misfit_two[...] = left.T.astype(jnp.bfloat16)
+    for i in range(blocks):
+        store(i).wait()
 
 
 def gradient_kernel(
@@ -323,6 +338,10 @@
         across(i).wait_send()
 
 
+def in_hbm(array):
+    return pltpu.with_memory_space_constraint(array, pltpu.HBM)
+
+
 def body(blk, line, codes, signals, dictionary):
     rows, count = codes.shape
     atoms, features = dictionary.shape
@@ -333,7 +352,7 @@
     links = len(bits_of(chips))
     part = atoms // line
     bf16, f32 = jnp.bfloat16, jnp.float32
-    any_spec = pl.BlockSpec(memory_space=pl.ANY)
+    hbm_spec = pl.BlockSpec(memory_space=pltpu.HBM)
     vmem_spec = pl.BlockSpec(memory_space=VMEM)
     flops = 2 * rows * count * features
     size = 2 * rows * count
@@ -344,12 +363,13 @@
             jax.ShapeDtypeStruct((blocks, features, width), bf16),
             jax.ShapeDtypeStruct((rows, features), bf16),
         ),
-        in_specs=[any_spec, vmem_spec, any_spec],
+        in_specs=[hbm_spec] * 3,
         out_specs=(vmem_spec, vmem_spec),
         scratch_shapes=[
             VMEM((blocks, rows, width), bf16),
+            VMEM((rows, features), bf16),
             VMEM((rows, features), f32),
-            DMA((blocks,)), DMA((HALVES,)),
+            DMA((blocks,)), DMA, DMA((HALVES,)),
             DMA((HALVES * max(chips - 1, 1),)), DMA((pieces,)),
             DMA((pieces,)), DMA((pieces,)),
         ],
@@ -358,26 +378,21 @@
         ),
         cost_estimate=pl.CostEstimate(flops=flops, bytes_accessed=2 * size, transcendentals=0),
         name="gather_atoms",
-    )(codes, signals, dictionary.T)
+    )(in_hbm(codes), in_hbm(signals), in_hbm(dictionary.T))
 
     fresh, misfit_two = pl.pallas_call(
-        update_kernel,
-        grid=(blocks,),
+        functools.partial(update_kernel, 4),
         out_shape=(
             jax.ShapeDtypeStruct((rows, count), bf16),
             jax.ShapeDtypeStruct((features, rows), bf16),
         ),
-        in_specs=[
-            pl.BlockSpec((rows, width), lambda i: (0, i)),
-            pl.BlockSpec((rows, features), lambda i: (0, 0)),
-            pl.BlockSpec((1, features, width), lambda i: (i, 0, 0)),
-            pl.BlockSpec((rows, features), lambda i: (0, 0)),
+        in_specs=[vmem_spec] * 4,
+        out_specs=(hbm_spec, vmem_spec),
+        scratch_shapes=[
+            VMEM((blocks, rows, width), bf16),
+            VMEM((rows, features), f32),
+            DMA((blocks,)),
         ],
-        out_specs=(
-            pl.BlockSpec((rows, width), lambda i: (0, i)),
-            pl.BlockSpec((features, rows), lambda i: (0, 0)),
-        ),
-        scratch_shapes=[VMEM((rows, features), f32)],
         compiler_params=pltpu.CompilerParams(vmem_limit_bytes=24 * 2**20),
         cost_estimate=pl.CostEstimate(flops=2 * flops, bytes_accessed=3 * size, transcendentals=0),
         name="update_codes",
@@ -386,7 +401,7 @@
     grad = pl.pallas_call(
         functools.partial(gradient_kernel, chips, line, float(rows * blk * line) ** -0.5),
         out_shape=jax.ShapeDtypeStruct((features, part), f32),
-        in_specs=[any_spec, vmem_spec],
+        in_specs=[hbm_spec, vmem_spec],
         out_specs=vmem_spec,
         scratch_shapes=[
             VMEM((blocks, rows, width), bf16),
@@ -405,7 +420,7 @@
         ),
         cost_estimate=pl.CostEstimate(flops=flops, bytes_accessed=2 * size, transcendentals=0),
         name="dictionary_gradient",
-    )(fresh, misfit_two)
+    )(in_hbm(fresh), misfit_two)
     return fresh, grad.T
 
 

time: 85.8 us -> 73.8 us (0.86)
  local copies, waits for them, and re-layouts: 7.34 us -> 0.72 us
  Pallas kernels: 77.3 us -> 72.2 us
    unnamed x11 -> x5, local copies, waits for them, and re-layouts: 7.34 us -> 0.72 us
    pallas_call x1, Pallas kernels: 9.67 us -> 4.11 us  [body(): pl.pallas_call(functools.partial(update_kernel, 4), out_shape=(jax.ShapeD...]
where the time goes in v2:
time: 73.8 us; the launch traced here: 73.6 us
  Pallas kernels  72.2 us (98%)
    pallas_call x1, Pallas kernels, body(): pl.pallas_call(functools.partial(gradient_kernel, chips, line, float(rows...  41.9 us
    pallas_call x1, Pallas kernels, body(): pl.pallas_call(functools.partial(gather_kernel, chips), out_shape=(jax.Sh...  26.2 us
    pallas_call x1, Pallas kernels, body(): pl.pallas_call(functools.partial(update_kernel, 4), out_shape=(jax.ShapeD...  4.11 us

profile of v2, /device:TPU:0, one launch (start us, length us, event | category | flops | bytes accessed | tf_op | source)
XLA Modules:
  0.0 73.6 jit_solution(16210454502949577712)
XLA Ops:
  0.6 0.0 copy-start.1
  0.6 0.0 copy-start
  0.6 26.2 %gather_atoms.1 = (bf16[16,192,768]{2,1,0:T(8,128)(2,1)S(1)}, bf16[192,192]{1,0:T(8,128)(2,1)S(1)}) custom-call(bf16[192,12288]{1,0:T(8,128)(2,1)} %codes.3, bf16[192,192]{1,0:T(8,128)(2,1)} %signals.3, bf16[192,1536]{1,0:T(8,128)(2,1)} %bitcast.3), custom_call_target="tpu_custom_call" | custom-call | flops 905969664 | bytes 9437184 | tf_op jit(solution)/shard_map/gather_atoms/pallas_call | solution.py:360
  26.8 0.0 copy-done.1
  26.8 0.0 copy-done
  26.8 4.1 %update_codes.1 = (bf16[192,12288]{1,0:T(8,128)(2,1)}, bf16[192,192]{1,0:T(8,128)(2,1)S(1)}) custom-call(bf16[192,12288]{1,0:T(8,128)(2,1)S(1)} %copy-done, bf16[192,192]{1,0:T(8,128)(2,1)S(1)} %copy-done.1, bf16[16,192,768]{2,1,0:T(8,128)(2,1)S(1)} %get-tuple-element.6.full, bf16[192,192]{1,0:T(8,128)(2,1)S(1)} %get-tuple-element.7.misfit), custom_call_target="tpu_custom_call" | custom-call | flops 1811939328 | bytes 14155776 | tf_op jit(solution)/shard_map/update_codes/pallas_call | solution.py:383
  31.0 41.9 %dictionary_gradient.1 = f32[192,384]{1,0:T(8,128)S(1)} custom-call(bf16[192,12288]{1,0:T(8,128)(2,1)} %get-tuple-element.12.fresh, bf16[192,192]{1,0:T(8,128)(2,1)S(1)} %get-tuple-element.9.misfit), custom_call_target="tpu_custom_call" | custom-call | flops 905969664 | bytes 9437184 | tf_op jit(solution)/shard_map/dictionary_gradient/pallas_call | solution.py:401
  72.9 0.7 copy.6
Async XLA Ops:
  0.6 26.2 %copy-start.1 = (bf16[192,192]{1,0:T(8,128)(2,1)S(1)}, bf16[192,192]{1,0:T(8,128)(2,1)}, u32[]{:S(2)}) copy-start(bf16[192,192]{1,0:T(8,128)(2,1)} %signals.3) | copy-start | bytes 221188
  0.6 26.2 %copy-start = (bf16[192,12288]{1,0:T(8,128)(2,1)S(1)}, bf16[192,12288]{1,0:T(8,128)(2,1)}, u32[]{:S(2)}) copy-start(bf16[192,12288]{1,0:T(8,128)(2,1)} %codes.3) | copy-start | bytes 14155780

commit v3 on v2

--- a/solution.py
+++ b/solution.py
@@ -166,7 +166,7 @@
         across(d, h, 0).wait_send()
 
 
-def update_kernel(together, codes, signals, full, misfit, fresh, misfit_two, made, total, store_sem):
+def update_kernel(together, codes, signals, full, misfit, fresh, made, misfit_two, total, store_sem):
     blocks, _, width = full.shape
 
     def store(i):
@@ -196,36 +196,38 @@
         store(i).wait()
 
 
+def slices_of(features):
+    unit = features // 12
+    ranges, start = [], 0
+    for size in (2 * unit, 2 * unit, unit, unit):
+        ranges.append([(start, size), (start + size, size)])
+        start += 2 * size
+    return ranges
+
+
+def gaps_of(chips):
+    bits = bits_of(chips)
+    return [
+        (d, b) for d in range(chips) for b in bits
+        if any(b in children(d, t, bits) for t in range(HALVES))
+    ]
+
+
 def gradient_kernel(
-    chips, line, scale, fresh, misfit, grad,
-    held, core_out, core_in, net_out, net_in, own, z_out, z_in,
-    load_sem, core_send, core_recv, net_send, net_recv, z_send, z_recv,
+    chips, line, scale, made, misfit, grad,
+    core_out, core_in, mine, net_out, net_in, own, z_out, z_in,
+    core_send, core_recv, net_send, net_recv, z_send, z_recv,
 ):
     bits = bits_of(chips)
+    gaps = gaps_of(chips)
+    slices = slices_of(grad.shape[0])
     me = lax.axis_index("blk")
     z = lax.axis_index("narrow")
     chip, core = me // CORES, me % CORES
     other = CORES * chip + 1 - core
-    width = held.shape[2]
+    width = made.shape[2]
     part = grad.shape[1]
 
-    order = sorted(
-        pieces_of(chips),
-        key=lambda p: (-ones(p[0]), len(children(p[0], p[1], bits)), p[0]),
-    )
-    uses = [(d, h, c) for d, h in order for c in (1, 0)]
-    entries = [(d, h, b) for d, h in order for b in children(d, h, bits)]
-
-    def load(slot):
-        d, h, c = uses[slot]
-        owner = CORES * flip(chip, d) + (core if c == 0 else 1 - core)
-        start = pl.multiple_of((owner * HALVES + h) * width, width)
-        return pltpu.make_async_copy(
-            fresh.at[:, pl.ds(start, width)], held.at[slot], load_sem.at[slot]
-        )
-
-    for slot in range(len(uses)):
-        load(slot).start()
     barrier = pltpu.get_barrier_semaphore()
     partners = [other] + [CORES * flip(chip, b) + core for b in bits]
     for partner in partners:
@@ -235,63 +237,84 @@
         pl.semaphore_signal(barrier, inc=1, device_id={"narrow": partner}, device_id_type=MESH)
 
     def term(d, h, c):
-        slot = uses.index((d, h, c))
-        load(slot).wait()
-        return jnp.dot(misfit[...], held[slot], preferred_element_type=jnp.float32)
-
-    def across(i):
+        owner = CORES * flip(chip, d) + (core if c == 0 else 1 - core)
+        return jnp.dot(misfit[...], made[owner * HALVES + h], preferred_element_type=jnp.float32)
+
+    def across(d, h):
+        i = d * HALVES + h
         return pltpu.make_async_remote_copy(
             core_out.at[i], core_in.at[i], core_send.at[i], core_recv.at[i],
             device_id={"blk": other}, device_id_type=MESH,
         )
 
-    def net(i, slot, b):
+    def hand_over(d):
+        for h in range(HALVES):
+            core_out[d * HALVES + h] = term(d, h, 1).astype(jnp.bfloat16)
+
+    def sum_cores(d):
+        for h in range(HALVES):
+            value = term(d, h, 0)
+            across(d, h).wait_recv()
+            mine[d, :, h * width:(h + 1) * width] = value + core_in[d * HALVES + h].astype(jnp.float32)
+
+    def net(d, k, t):
+        b = toward(d, t)
+        start, size = slices[k][t]
+        gap = gaps.index((d ^ b, b))
+        rows = pl.ds(start, size)
         return pltpu.make_async_remote_copy(
-            net_out.at[i], net_in.at[slot], net_send.at[i], net_recv.at[slot],
+            net_out.at[d - 1, rows], net_in.at[gap, rows],
+            net_send.at[d - 1, k, t], net_recv.at[gap, k, t],
             device_id={"blk": CORES * flip(chip, b) + core}, device_id_type=MESH,
         )
 
-    def hand_over(i):
-        d, h = order[i]
-        core_out[i] = term(d, h, 1).astype(jnp.bfloat16)
-        if i == 0:
-            pl.semaphore_wait(barrier, len(partners) + len(beside))
-        across(i).start()
-
-    ahead = min(2, len(order))
-    for i in range(ahead):
-        hand_over(i)
-    sends = []
-    for i, (d, h) in enumerate(order):
-        if i + ahead < len(order):
-            hand_over(i + ahead)
-        value = term(d, h, 0)
-        across(i).wait_recv()
-        value += core_in[i].astype(jnp.float32)
-        for b in children(d, h, bits):
-            slot = entries.index((d, h, b))
-            net(0, slot, b).wait_recv()
-            value += net_in[slot].astype(jnp.float32)
-        if d:
-            b = toward(d, h)
-            net_out[i] = value.astype(jnp.bfloat16)
-            copy = net(i, entries.index((d ^ b, h, b)), b)
-            copy.start()
-            sends.append(copy)
-        else:
-            for j in range(width // part):
-                own[h * (width // part) + j] = value[:, j * part:(j + 1) * part]
-
-    def z_copy(side, t):
+    def summed(d, k, t):
+        start, size = slices[k][t]
+        value = mine[d, start:start + size]
+        for b in children(d, t, bits):
+            gap = gaps.index((d, b))
+            rows = pl.ds(start, size)
+            pltpu.make_async_remote_copy(
+                net_out.at[0, rows], net_in.at[gap, rows],
+                net_send.at[0, k, t], net_recv.at[gap, k, t],
+                device_id={"blk": other}, device_id_type=MESH,
+            ).wait_recv()
+            value += net_in[gap, start:start + size].astype(jnp.float32)
+        return value
+
+    def pass_on(d, k, t):
+        start, size = slices[k][t]
+        net_out[d - 1, start:start + size] = summed(d, k, t).astype(jnp.bfloat16)
+        net(d, k, t).start()
+
+    away = sorted(((d, t) for d in range(1, chips) for t in range(HALVES)), key=lambda p: -ones(p[0]))
+    firsts = [p for p in away if not children(*p, bits)]
+    relays = [p for p in away if children(*p, bits)]
+
+    def arrive(k):
+        for t in range(HALVES):
+            start, size = slices[k][t]
+            value = summed(0, k, t)
+            for j in range(line):
+                own[j, start:start + size] = value[:, j * part:(j + 1) * part]
+
+    def span(k):
+        start = slices[k][0][0]
+        return start, sum(size for _, size in slices[k])
+
+    def z_copy(k, side, t):
+        rows = pl.ds(*span(k))
         return pltpu.make_async_remote_copy(
-            z_out.at[side, t], z_in.at[side, t - 1],
-            z_send.at[side, t], z_recv.at[side, t - 1],
+            z_out.at[side, t, rows], z_in.at[side, t - 1, rows],
+            z_send.at[side, t, k], z_recv.at[side, t - 1, k],
             device_id={"narrow": z + 1 if side == 0 else z - 1}, device_id_type=MESH,
         )
 
-    def z_arrived(side, t):
+    def z_arrived(k, side, t):
+        rows = pl.ds(*span(k))
         pltpu.make_async_remote_copy(
-            z_out.at[side, 0], z_in.at[side, t], z_send.at[side, 0], z_recv.at[side, t],
+            z_out.at[side, 0, rows], z_in.at[side, t, rows],
+            z_send.at[side, 0, k], z_recv.at[side, t, k],
             device_id={"narrow": z - 1 if side == 0 else z + 1}, device_id_type=MESH,
         ).wait_recv()
 
@@ -301,41 +324,81 @@
     def in_line(side, t):
         return z + t < line if side == 0 else z - t >= 0
 
-    for t in range(line - 1, 0, -1):
+    def z_step(k, t):
+        start, size = span(k)
+        rows = pl.ds(start, size)
         for side in range(2):
             @pl.when(in_line(side, t))
             def _():
-                mine = own[z + t if side == 0 else z - t]
+                value = own[z + t if side == 0 else z - t, rows]
 
                 @pl.when(has_behind(side))
                 def _():
-                    z_arrived(side, t)
-                    z_out[side, t] = (mine + z_in[side, t].astype(jnp.float32)).astype(jnp.bfloat16)
+                    z_arrived(k, side, t)
+                    z_out[side, t, rows] = (
+                        value + z_in[side, t, rows].astype(jnp.float32)
+                    ).astype(jnp.bfloat16)
 
                 @pl.when(jnp.logical_not(has_behind(side)))
                 def _():
-                    z_out[side, t] = mine.astype(jnp.bfloat16)
-
-                z_copy(side, t).start()
-
-    grad[...] = own[z]
-    if line > 1:
+                    z_out[side, t, rows] = value.astype(jnp.bfloat16)
+
+                z_copy(k, side, t).start()
+
+    def z_finish(k):
+        rows = pl.ds(*span(k))
+        grad[rows] = own[z, rows] * scale
         for side in range(2):
             @pl.when(has_behind(side))
             def _():
-                z_arrived(side, 0)
-                grad[...] += z_in[side, 0].astype(jnp.float32)
-    grad[...] = grad[...] * scale
-
-    for t in range(line - 1, 0, -1):
-        for side in range(2):
-            @pl.when(in_line(side, t))
-            def _():
-                z_copy(side, t).wait_send()
-    for copy in sends:
-        copy.wait_send()
-    for i in range(len(order)):
-        across(i).wait_send()
+                z_arrived(k, side, 0)
+                grad[rows] += z_in[side, 0, rows].astype(jnp.float32) * scale
+
+    order = sorted(range(chips), key=lambda d: (-ones(d), d))
+    hand_over(order[0])
+    pl.semaphore_wait(barrier, len(partners) + len(beside))
+    for h in range(HALVES):
+        across(order[0], h).start()
+    for i, d in enumerate(order):
+        if i + 1 < chips:
+            hand_over(order[i + 1])
+            for h in range(HALVES):
+                across(order[i + 1], h).start()
+        sum_cores(d)
+        for e, t in firsts:
+            if e == d:
+                pass_on(d, 0, t)
+    count = len(slices)
+    for k in range(1, min(2, count)):
+        for d, t in firsts:
+            pass_on(d, k, t)
+    for now in range(count + line):
+        if now < count:
+            for d, t in relays:
+                pass_on(d, now, t)
+        if now + 2 < count:
+            for d, t in firsts:
+                pass_on(d, now + 2, t)
+        if 1 <= now <= count:
+            arrive(now - 1)
+        for k in range(count):
+            t = line - 1 - (now - 1 - k)
+            if 1 <= t <= line - 1:
+                z_step(k, t)
+            elif t == 0:
+                z_finish(k)
+
+    for k in range(count):
+        for d, t in away:
+            net(d, k, t).wait_send()
+        for t in range(1, line):
+            for side in range(2):
+                @pl.when(in_line(side, t))
+                def _():
+                    z_copy(k, side, t).wait_send()
+    for d in range(chips):
+        for h in range(HALVES):
+            across(d, h).wait_send()
 
 
 def in_hbm(array):
@@ -349,7 +412,6 @@
     width = atoms // HALVES
     blocks = blk * HALVES
     pieces = chips * HALVES
-    links = len(bits_of(chips))
     part = atoms // line
     bf16, f32 = jnp.bfloat16, jnp.float32
     hbm_spec = pl.BlockSpec(memory_space=pltpu.HBM)
@@ -380,16 +442,16 @@
         name="gather_atoms",
     )(in_hbm(codes), in_hbm(signals), in_hbm(dictionary.T))
 
-    fresh, misfit_two = pl.pallas_call(
+    fresh, made, misfit_two = pl.pallas_call(
         functools.partial(update_kernel, 4),
         out_shape=(
             jax.ShapeDtypeStruct((rows, count), bf16),
+            jax.ShapeDtypeStruct((blocks, rows, width), bf16),
             jax.ShapeDtypeStruct((features, rows), bf16),
         ),
         in_specs=[vmem_spec] * 4,
-        out_specs=(hbm_spec, vmem_spec),
+        out_specs=(hbm_spec, vmem_spec, vmem_spec),
         scratch_shapes=[
-            VMEM((blocks, rows, width), bf16),
             VMEM((rows, features), f32),
             DMA((blocks,)),
         ],
@@ -398,29 +460,33 @@
         name="update_codes",
     )(codes, signals, full, misfit)
 
+    gaps = max(len(gaps_of(chips)), 1)
+    far = max(chips - 1, 1)
+    count_of = len(slices_of(features))
     grad = pl.pallas_call(
         functools.partial(gradient_kernel, chips, line, float(rows * blk * line) ** -0.5),
         out_shape=jax.ShapeDtypeStruct((features, part), f32),
-        in_specs=[hbm_spec, vmem_spec],
+        in_specs=[vmem_spec] * 2,
         out_specs=vmem_spec,
         scratch_shapes=[
-            VMEM((blocks, rows, width), bf16),
             VMEM((pieces, features, width), bf16),
             VMEM((pieces, features, width), bf16),
-            VMEM((pieces, features, width), bf16),
-            VMEM((max(HALVES * (chips - 1), 1), features, width), bf16),
+            VMEM((chips, features, atoms), f32),
+            VMEM((far, features, atoms), bf16),
+            VMEM((gaps, features, atoms), bf16),
             VMEM((line, features, part), f32),
             VMEM((2, line, features, part), bf16),
             VMEM((2, line, features, part), bf16),
-            DMA((blocks,)), DMA((pieces,)), DMA((pieces,)), DMA((pieces,)),
-            DMA((max(HALVES * (chips - 1), 1),)), DMA((2, line)), DMA((2, line)),
+            DMA((pieces,)), DMA((pieces,)),
+            DMA((far, count_of, HALVES)), DMA((gaps, count_of, HALVES)),
+            DMA((2, line, count_of)), DMA((2, line, count_of)),
         ],
         compiler_params=pltpu.CompilerParams(
-            collective_id=1, has_side_effects=True, vmem_limit_bytes=40 * 2**20
+            collective_id=1, has_side_effects=True, vmem_limit_bytes=32 * 2**20
         ),
         cost_estimate=pl.CostEstimate(flops=flops, bytes_accessed=2 * size, transcendentals=0),
         name="dictionary_gradient",
-    )(in_hbm(fresh), misfit_two)
+    )(made, misfit_two)
     return fresh, grad.T
 
 

time: 73.8 us -> 74.1 us (level)
  no operation moved by 1% of the time
where the time goes in v3:
time: 74.1 us; the launch traced here: 74 us
  Pallas kernels  72.6 us (98%)
    pallas_call x1, Pallas kernels, body(): pl.pallas_call(functools.partial(gradient_kernel, chips, line, float(rows...  42.3 us
    pallas_call x1, Pallas kernels, body(): pl.pallas_call(functools.partial(gather_kernel, chips), out_shape=(jax.Sh...  26.2 us
    pallas_call x1, Pallas kernels, body(): pl.pallas_call(functools.partial(update_kernel, 4), out_shape=(jax.ShapeD...  4.11 us

profile of v3, /device:TPU:0, one launch (start us, length us, event | category | flops | bytes accessed | tf_op | source)
XLA Modules:
  0.0 74.0 jit_solution(8067476142547683069)
XLA Ops:
  0.6 0.0 copy-start.1
  0.6 0.0 copy-start
  0.6 26.2 %gather_atoms.1 = (bf16[16,192,768]{2,1,0:T(8,128)(2,1)S(1)}, bf16[192,192]{1,0:T(8,128)(2,1)S(1)}) custom-call(bf16[192,12288]{1,0:T(8,128)(2,1)} %codes.3, bf16[192,192]{1,0:T(8,128)(2,1)} %signals.3, bf16[192,1536]{1,0:T(8,128)(2,1)} %bitcast.3), custom_call_target="tpu_custom_call" | custom-call | flops 905969664 | bytes 9437184 | tf_op jit(solution)/shard_map/gather_atoms/pallas_call | solution.py:422
  26.8 0.0 copy-done.1
  26.8 0.0 copy-done
  26.8 4.1 %update_codes.1 = (bf16[192,12288]{1,0:T(8,128)(2,1)}, bf16[16,192,768]{2,1,0:T(8,128)(2,1)S(1)}, bf16[192,192]{1,0:T(8,128)(2,1)S(1)}) custom-call(bf16[192,12288]{1,0:T(8,128)(2,1)S(1)} %copy-done, bf16[192,192]{1,0:T(8,128)(2,1)S(1)} %copy-done.1, bf16[16,192,768]{2,1,0:T(8,128)(2,1)S(1)} %get-tuple-element.7.full, ...), custom_call_target="tpu_custom_call" | custom-call | flops 1811939328 | bytes 14155776 | tf_op jit(solution)/shard_map/update_codes/pallas_call | solution.py:445
  31.0 42.3 %dictionary_gradient.1 = f32[192,384]{1,0:T(8,128)S(1)} custom-call(bf16[16,192,768]{2,1,0:T(8,128)(2,1)S(1)} %get-tuple-element.10.made, bf16[192,192]{1,0:T(8,128)(2,1)S(1)} %get-tuple-element.11.misfit), custom_call_target="tpu_custom_call" | custom-call | flops 905969664 | bytes 9437184 | tf_op jit(solution)/shard_map/dictionary_gradient/pallas_call | solution.py:466
  73.2 0.7 copy.6
Async XLA Ops:
  0.6 26.2 %copy-start.1 = (bf16[192,192]{1,0:T(8,128)(2,1)S(1)}, bf16[192,192]{1,0:T(8,128)(2,1)}, u32[]{:S(2)}) copy-start(bf16[192,192]{1,0:T(8,128)(2,1)} %signals.3) | copy-start | bytes 221188
  0.6 26.2 %copy-start = (bf16[192,12288]{1,0:T(8,128)(2,1)S(1)}, bf16[192,12288]{1,0:T(8,128)(2,1)}, u32[]{:S(2)}) copy-start(bf16[192,12288]{1,0:T(8,128)(2,1)} %codes.3) | copy-start | bytes 14155780

commit v4 on v3

--- a/solution.py
+++ b/solution.py
@@ -199,7 +199,7 @@
 def slices_of(features):
     unit = features // 12
     ranges, start = [], 0
-    for size in (2 * unit, 2 * unit, unit, unit):
+    for size in (unit, 2 * unit, 2 * unit, unit):
         ranges.append([(start, size), (start + size, size)])
         start += 2 * size
     return ranges
@@ -240,22 +240,20 @@
         owner = CORES * flip(chip, d) + (core if c == 0 else 1 - core)
         return jnp.dot(misfit[...], made[owner * HALVES + h], preferred_element_type=jnp.float32)
 
-    def across(d, h):
-        i = d * HALVES + h
+    def span(k):
+        start = slices[k][0][0]
+        return start, sum(size for _, size in slices[k])
+
+    def across(d, k):
+        rows = pl.ds(*span(k))
         return pltpu.make_async_remote_copy(
-            core_out.at[i], core_in.at[i], core_send.at[i], core_recv.at[i],
+            core_out.at[d, rows], core_in.at[d, rows], core_send.at[d, k], core_recv.at[d, k],
             device_id={"blk": other}, device_id_type=MESH,
         )
 
-    def hand_over(d):
+    def compute(into, d, c):
         for h in range(HALVES):
-            core_out[d * HALVES + h] = term(d, h, 1).astype(jnp.bfloat16)
-
-    def sum_cores(d):
-        for h in range(HALVES):
-            value = term(d, h, 0)
-            across(d, h).wait_recv()
-            mine[d, :, h * width:(h + 1) * width] = value + core_in[d * HALVES + h].astype(jnp.float32)
+            into[d, :, h * width:(h + 1) * width] = term(d, h, c).astype(into.dtype)
 
     def net(d, k, t):
         b = toward(d, t)
@@ -270,7 +268,7 @@
 
     def summed(d, k, t):
         start, size = slices[k][t]
-        value = mine[d, start:start + size]
+        value = mine[d, start:start + size] + core_in[d, start:start + size].astype(jnp.float32)
         for b in children(d, t, bits):
             gap = gaps.index((d, b))
             rows = pl.ds(start, size)
@@ -298,10 +296,6 @@
             for j in range(line):
                 own[j, start:start + size] = value[:, j * part:(j + 1) * part]
 
-    def span(k):
-        start = slices[k][0][0]
-        return start, sum(size for _, size in slices[k])
-
     def z_copy(k, side, t):
         rows = pl.ds(*span(k))
         return pltpu.make_async_remote_copy(
@@ -355,30 +349,34 @@
                 grad[rows] += z_in[side, 0, rows].astype(jnp.float32) * scale
 
     order = sorted(range(chips), key=lambda d: (-ones(d), d))
-    hand_over(order[0])
-    pl.semaphore_wait(barrier, len(partners) + len(beside))
-    for h in range(HALVES):
-        across(order[0], h).start()
+    count = len(slices)
     for i, d in enumerate(order):
-        if i + 1 < chips:
-            hand_over(order[i + 1])
-            for h in range(HALVES):
-                across(order[i + 1], h).start()
-        sum_cores(d)
+        compute(core_out, d, 1)
+        if i == 0:
+            pl.semaphore_wait(barrier, len(partners) + len(beside))
+        across(d, 0).start()
+    for d in order:
+        across(d, 1).start()
+
+    def begin(d, k):
+        across(d, k).wait_recv()
         for e, t in firsts:
             if e == d:
-                pass_on(d, 0, t)
-    count = len(slices)
-    for k in range(1, min(2, count)):
-        for d, t in firsts:
-            pass_on(d, k, t)
+                pass_on(d, k, t)
+
+    for d in order:
+        compute(mine, d, 0)
+        begin(d, 0)
     for now in range(count + line):
+        if now + 2 < count:
+            for d in order:
+                across(d, now + 2).start()
         if now < count:
             for d, t in relays:
                 pass_on(d, now, t)
-        if now + 2 < count:
-            for d, t in firsts:
-                pass_on(d, now + 2, t)
+        if now + 1 < count:
+            for d in order:
+                begin(d, now + 1)
         if 1 <= now <= count:
             arrive(now - 1)
         for k in range(count):
@@ -396,9 +394,9 @@
                 @pl.when(in_line(side, t))
                 def _():
                     z_copy(k, side, t).wait_send()
-    for d in range(chips):
-        for h in range(HALVES):
-            across(d, h).wait_send()
+    for k in range(count):
+        for d in order:
+            across(d, k).wait_send()
 
 
 def in_hbm(array):
@@ -469,15 +467,15 @@
         in_specs=[vmem_spec] * 2,
         out_specs=vmem_spec,
         scratch_shapes=[
-            VMEM((pieces, features, width), bf16),
-            VMEM((pieces, features, width), bf16),
+            VMEM((chips, features, atoms), bf16),
+            VMEM((chips, features, atoms), bf16),
             VMEM((chips, features, atoms), f32),
             VMEM((far, features, atoms), bf16),
             VMEM((gaps, features, atoms), bf16),
             VMEM((line, features, part), f32),
             VMEM((2, line, features, part), bf16),
             VMEM((2, line, features, part), bf16),
-            DMA((pieces,)), DMA((pieces,)),
+            DMA((chips, count_of)), DMA((chips, count_of)),
             DMA((far, count_of, HALVES)), DMA((gaps, count_of, HALVES)),
             DMA((2, line, count_of)), DMA((2, line, count_of)),
         ],

time: 74.1 us -> 73.5 us (level)
  no operation moved by 1% of the time
where the time goes in v4:
time: 73.5 us; the launch traced here: 73.4 us
  Pallas kernels  71.9 us (98%)
    pallas_call x1, Pallas kernels, body(): pl.pallas_call(functools.partial(gradient_kernel, chips, line, float(rows...  41.7 us
    pallas_call x1, Pallas kernels, body(): pl.pallas_call(functools.partial(gather_kernel, chips), out_shape=(jax.Sh...  26.2 us
    pallas_call x1, Pallas kernels, body(): pl.pallas_call(functools.partial(update_kernel, 4), out_shape=(jax.ShapeD...  4.11 us

profile of v4, /device:TPU:0, one launch (start us, length us, event | category | flops | bytes accessed | tf_op | source)
XLA Modules:
  0.0 73.4 jit_solution(6317378239579255343)
XLA Ops:
  0.6 0.0 copy-start.1
  0.6 0.0 copy-start
  0.6 26.2 %gather_atoms.1 = (bf16[16,192,768]{2,1,0:T(8,128)(2,1)S(1)}, bf16[192,192]{1,0:T(8,128)(2,1)S(1)}) custom-call(bf16[192,12288]{1,0:T(8,128)(2,1)} %codes.3, bf16[192,192]{1,0:T(8,128)(2,1)} %signals.3, bf16[192,1536]{1,0:T(8,128)(2,1)} %bitcast.3), custom_call_target="tpu_custom_call" | custom-call | flops 905969664 | bytes 9437184 | tf_op jit(solution)/shard_map/gather_atoms/pallas_call | solution.py:420
  26.8 0.0 copy-done.1
  26.8 0.0 copy-done
  26.8 4.1 %update_codes.1 = (bf16[192,12288]{1,0:T(8,128)(2,1)}, bf16[16,192,768]{2,1,0:T(8,128)(2,1)S(1)}, bf16[192,192]{1,0:T(8,128)(2,1)S(1)}) custom-call(bf16[192,12288]{1,0:T(8,128)(2,1)S(1)} %copy-done, bf16[192,192]{1,0:T(8,128)(2,1)S(1)} %copy-done.1, bf16[16,192,768]{2,1,0:T(8,128)(2,1)S(1)} %get-tuple-element.7.full, ...), custom_call_target="tpu_custom_call" | custom-call | flops 1811939328 | bytes 14155776 | tf_op jit(solution)/shard_map/update_codes/pallas_call | solution.py:443
  31.0 41.7 %dictionary_gradient.1 = f32[192,384]{1,0:T(8,128)S(1)} custom-call(bf16[16,192,768]{2,1,0:T(8,128)(2,1)S(1)} %get-tuple-element.10.made, bf16[192,192]{1,0:T(8,128)(2,1)S(1)} %get-tuple-element.11.misfit), custom_call_target="tpu_custom_call" | custom-call | flops 905969664 | bytes 9437184 | tf_op jit(solution)/shard_map/dictionary_gradient/pallas_call | solution.py:464
  72.6 0.7 copy.6
Async XLA Ops:
  0.6 26.2 %copy-start.1 = (bf16[192,192]{1,0:T(8,128)(2,1)S(1)}, bf16[192,192]{1,0:T(8,128)(2,1)}, u32[]{:S(2)}) copy-start(bf16[192,192]{1,0:T(8,128)(2,1)} %signals.3) | copy-start | bytes 221188
  0.6 26.2 %copy-start = (bf16[192,12288]{1,0:T(8,128)(2,1)S(1)}, bf16[192,12288]{1,0:T(8,128)(2,1)}, u32[]{:S(2)}) copy-start(bf16[192,12288]{1,0:T(8,128)(2,1)} %codes.3) | copy-start | bytes 14155780

commit v5 on v4

--- a/solution.py
+++ b/solution.py
@@ -232,7 +232,7 @@
     partners = [other] + [CORES * flip(chip, b) + core for b in bits]
     for partner in partners:
         pl.semaphore_signal(barrier, inc=1, device_id={"blk": partner}, device_id_type=MESH)
-    beside = [(z + 1) % line, (z + line - 1) % line] if line > 1 else []
+    beside = [(z + t) % line for t in range(1, line)]
     for partner in beside:
         pl.semaphore_signal(barrier, inc=1, device_id={"narrow": partner}, device_id_type=MESH)
 
@@ -296,57 +296,26 @@
             for j in range(line):
                 own[j, start:start + size] = value[:, j * part:(j + 1) * part]
 
-    def z_copy(k, side, t):
+    def z_copy(k, t):
         rows = pl.ds(*span(k))
         return pltpu.make_async_remote_copy(
-            z_out.at[side, t, rows], z_in.at[side, t - 1, rows],
-            z_send.at[side, t, k], z_recv.at[side, t - 1, k],
-            device_id={"narrow": z + 1 if side == 0 else z - 1}, device_id_type=MESH,
-        )
-
-    def z_arrived(k, side, t):
+            z_out.at[t - 1, rows], z_in.at[t - 1, rows], z_send.at[t - 1, k], z_recv.at[t - 1, k],
+            device_id={"narrow": (z + t) % line}, device_id_type=MESH,
+        )
+
+    def spread(k):
         rows = pl.ds(*span(k))
-        pltpu.make_async_remote_copy(
-            z_out.at[side, 0, rows], z_in.at[side, t, rows],
-            z_send.at[side, 0, k], z_recv.at[side, t, k],
-            device_id={"narrow": z - 1 if side == 0 else z + 1}, device_id_type=MESH,
-        ).wait_recv()
-
-    def has_behind(side):
-        return z >= 1 if side == 0 else z <= line - 2
-
-    def in_line(side, t):
-        return z + t < line if side == 0 else z - t >= 0
-
-    def z_step(k, t):
-        start, size = span(k)
-        rows = pl.ds(start, size)
-        for side in range(2):
-            @pl.when(in_line(side, t))
-            def _():
-                value = own[z + t if side == 0 else z - t, rows]
-
-                @pl.when(has_behind(side))
-                def _():
-                    z_arrived(k, side, t)
-                    z_out[side, t, rows] = (
-                        value + z_in[side, t, rows].astype(jnp.float32)
-                    ).astype(jnp.bfloat16)
-
-                @pl.when(jnp.logical_not(has_behind(side)))
-                def _():
-                    z_out[side, t, rows] = value.astype(jnp.bfloat16)
-
-                z_copy(k, side, t).start()
-
-    def z_finish(k):
+        for t in range(line - 1, 0, -1):
+            z_out[t - 1, rows] = own[(z + t) % line, rows].astype(jnp.bfloat16)
+            z_copy(k, t).start()
+
+    def finish(k):
         rows = pl.ds(*span(k))
-        grad[rows] = own[z, rows] * scale
-        for side in range(2):
-            @pl.when(has_behind(side))
-            def _():
-                z_arrived(k, side, 0)
-                grad[rows] += z_in[side, 0, rows].astype(jnp.float32) * scale
+        value = own[z, rows]
+        for t in range(1, line):
+            z_copy(k, t).wait_recv()
+            value += z_in[t - 1, rows].astype(jnp.float32)
+        grad[rows] = value * scale
 
     order = sorted(range(chips), key=lambda d: (-ones(d), d))
     count = len(slices)
@@ -367,7 +336,7 @@
     for d in order:
         compute(mine, d, 0)
         begin(d, 0)
-    for now in range(count + line):
+    for now in range(count + 3):
         if now + 2 < count:
             for d in order:
                 across(d, now + 2).start()
@@ -379,24 +348,17 @@
                 begin(d, now + 1)
         if 1 <= now <= count:
             arrive(now - 1)
-        for k in range(count):
-            t = line - 1 - (now - 1 - k)
-            if 1 <= t <= line - 1:
-                z_step(k, t)
-            elif t == 0:
-                z_finish(k)
+            spread(now - 1)
+        if now >= 3:
+            finish(now - 3)
 
     for k in range(count):
+        for d in order:
+            across(d, k).wait_send()
         for d, t in away:
             net(d, k, t).wait_send()
         for t in range(1, line):
-            for side in range(2):
-                @pl.when(in_line(side, t))
-                def _():
-                    z_copy(k, side, t).wait_send()
-    for k in range(count):
-        for d in order:
-            across(d, k).wait_send()
+            z_copy(k, t).wait_send()
 
 
 def in_hbm(array):
@@ -473,11 +435,11 @@
             VMEM((far, features, atoms), bf16),
             VMEM((gaps, features, atoms), bf16),
             VMEM((line, features, part), f32),
-            VMEM((2, line, features, part), bf16),
-            VMEM((2, line, features, part), bf16),
+            VMEM((max(line - 1, 1), features, part), bf16),
+            VMEM((max(line - 1, 1), features, part), bf16),
             DMA((chips, count_of)), DMA((chips, count_of)),
             DMA((far, count_of, HALVES)), DMA((gaps, count_of, HALVES)),
-            DMA((2, line, count_of)), DMA((2, line, count_of)),
+            DMA((max(line - 1, 1), count_of)), DMA((max(line - 1, 1), count_of)),
         ],
         compiler_params=pltpu.CompilerParams(
             collective_id=1, has_side_effects=True, vmem_limit_bytes=32 * 2**20

time: 73.5 us -> 65.3 us (0.89)
  Pallas kernels: 71.9 us -> 63.8 us
    pallas_call x1, Pallas kernels: 41.7 us -> 33.5 us  [body(): pl.pallas_call(functools.partial(gradient_kernel, chips, line, float(rows...]
where the time goes in v5:
time: 65.3 us; the launch traced here: 65.2 us
  Pallas kernels  63.8 us (98%)
  local copies, waits for them, and re-layouts  0.72 us (1%)
  between operations  0.69 us (1%)
    pallas_call x1, Pallas kernels, body(): pl.pallas_call(functools.partial(gradient_kernel, chips, line, float(rows...  33.5 us
    pallas_call x1, Pallas kernels, body(): pl.pallas_call(functools.partial(gather_kernel, chips), out_shape=(jax.Sh...  26.2 us
    pallas_call x1, Pallas kernels, body(): pl.pallas_call(functools.partial(update_kernel, 4), out_shape=(jax.ShapeD...  4.11 us

profile of v5, /device:TPU:0, one launch (start us, length us, event | category | flops | bytes accessed | tf_op | source)
XLA Modules:
  0.0 65.2 jit_solution(5682709086877582289)
XLA Ops:
  0.6 0.0 copy-start.1
  0.6 0.0 copy-start
  0.6 26.2 %gather_atoms.1 = (bf16[16,192,768]{2,1,0:T(8,128)(2,1)S(1)}, bf16[192,192]{1,0:T(8,128)(2,1)S(1)}) custom-call(bf16[192,12288]{1,0:T(8,128)(2,1)} %codes.3, bf16[192,192]{1,0:T(8,128)(2,1)} %signals.3, bf16[192,1536]{1,0:T(8,128)(2,1)} %bitcast.3), custom_call_target="tpu_custom_call" | custom-call | flops 905969664 | bytes 9437184 | tf_op jit(solution)/shard_map/gather_atoms/pallas_call | solution.py:382
  26.8 0.0 copy-done.1
  26.8 0.0 copy-done
  26.8 4.1 %update_codes.1 = (bf16[192,12288]{1,0:T(8,128)(2,1)}, bf16[16,192,768]{2,1,0:T(8,128)(2,1)S(1)}, bf16[192,192]{1,0:T(8,128)(2,1)S(1)}) custom-call(bf16[192,12288]{1,0:T(8,128)(2,1)S(1)} %copy-done, bf16[192,192]{1,0:T(8,128)(2,1)S(1)} %copy-done.1, bf16[16,192,768]{2,1,0:T(8,128)(2,1)S(1)} %get-tuple-element.7.full, ...), custom_call_target="tpu_custom_call" | custom-call | flops 1811939328 | bytes 14155776 | tf_op jit(solution)/shard_map/update_codes/pallas_call | solution.py:405
  31.0 33.5 %dictionary_gradient.1 = f32[192,384]{1,0:T(8,128)S(1)} custom-call(bf16[16,192,768]{2,1,0:T(8,128)(2,1)S(1)} %get-tuple-element.10.made, bf16[192,192]{1,0:T(8,128)(2,1)S(1)} %get-tuple-element.11.misfit), custom_call_target="tpu_custom_call" | custom-call | flops 905969664 | bytes 9437184 | tf_op jit(solution)/shard_map/dictionary_gradient/pallas_call | solution.py:426
  64.5 0.7 %copy.6 = f32[384,192]{0,1:T(8,128)} copy(f32[384,192]{0,1:T(8,128)S(1)} %bitcast.2) | data formatting | bytes 589824
Async XLA Ops:
  0.6 26.2 %copy-start.1 = (bf16[192,192]{1,0:T(8,128)(2,1)S(1)}, bf16[192,192]{1,0:T(8,128)(2,1)}, u32[]{:S(2)}) copy-start(bf16[192,192]{1,0:T(8,128)(2,1)} %signals.3) | copy-start | bytes 221188
  0.6 26.2 %copy-start = (bf16[192,12288]{1,0:T(8,128)(2,1)S(1)}, bf16[192,12288]{1,0:T(8,128)(2,1)}, u32[]{:S(2)}) copy-start(bf16[192,12288]{1,0:T(8,128)(2,1)} %codes.3) | copy-start | bytes 14155780

commit v6 on v5

--- a/solution.py
+++ b/solution.py
@@ -10,7 +10,8 @@
 MESH = pl.DeviceIdType.MESH
 VMEM = pltpu.VMEM
 DMA = pltpu.SemaphoreType.DMA
-HALVES = 2
+TREES = 2
+UNITS = 6
 CORES = 2
 
 
@@ -47,123 +48,159 @@
     return [b for b in bits if d == 0 or (b < low(d) if half == 0 else b > high(d))]
 
 
-def pieces_of(chips):
-    return [(d, h) for d in range(chips) for h in range(HALVES)]
-
-
 def nt_dot(a, b):
     return lax.dot_general(a, b, (((1,), (1,)), ((), ())), preferred_element_type=jnp.float32)
 
 
 def gather_kernel(
-    chips, codes, signals, atoms, full, misfit, held, target, total,
-    load_sem, target_sem, atom_sem, net_send, net_recv, core_send, core_recv,
+    chips, line, codes, signals, atoms, full, misfit, held, target, total,
+    load_sem, target_sem, atom_sem, net_send, net_recv, pair_send, core_send, core_recv,
 ):
     bits = bits_of(chips)
     me = lax.axis_index("blk")
+    z = lax.axis_index("narrow")
+    odd = z % 2
     chip, core = me // CORES, me % CORES
     other = CORES * chip + 1 - core
     width = full.shape[2]
-
-    def owner(d, c):
-        return CORES * flip(chip, d) + c
-
-    order = sorted(
-        pieces_of(chips),
-        key=lambda p: (ones(p[0]), -len(children(p[0], p[1], bits)), p[0]),
-    )
-    uses = [(d, h, c) for d, h in order for c in range(CORES)]
-
-    def atom_copy(h):
-        return pltpu.make_async_copy(
-            atoms.at[:, pl.ds(h * width, width)], full.at[me * HALVES + h], atom_sem.at[h]
-        )
-
-    def block(d, h, c):
-        return owner(d, core if c == 0 else 1 - core) * HALVES + h
+    paired = line % 2 == 0
+    lead, rest, late = ([2, 3], [0, 1], [4, 5]) if paired else ([], list(range(UNITS)), [])
+
+    def branches(d, u):
+        return [] if u in late else children(d, u % TREES, bits)
+
+    def block(d, u, c):
+        unit = u
+        if u in lead:
+            unit = u + 2 * odd
+        if u in late:
+            unit = u - 2 * odd
+        return (CORES * flip(chip, d) + (core if c == 0 else 1 - core)) * UNITS + unit
+
+    def key(piece):
+        return ones(piece[0]), -len(branches(*piece)), piece
+
+    def sort(units, hops):
+        return sorted([(d, u) for d in range(1, chips) if ones(d) in hops for u in units], key=key)
+
+    near, distant = [1], range(2, chips)
+    order = sort(lead, near) + sort(lead, distant) + sort(rest, near) + sort(late, near)
+    order += sort(late, distant) + sort(rest, distant)
+    own = [(0, u) for u in range(UNITS)]
+    uses = [(d, u, c) for c in range(CORES) for d, u in own]
+    uses += [(d, u, c) for d, u in order for c in range(CORES)]
+
+    atom_copies = [
+        pltpu.make_async_copy(
+            atoms.at[:, pl.ds(u * width, width)], full.at[me * UNITS + u], atom_sem.at[u]
+        )
+        for u in range(UNITS)
+    ]
+    for copy in atom_copies:
+        copy.start()
+    partners = [{"blk": other}] + [{"blk": CORES * flip(chip, b) + core} for b in bits]
+    if paired:
+        partners.append({"narrow": z + 1 - 2 * odd})
+    barrier = pltpu.get_barrier_semaphore()
+    for partner in partners:
+        pl.semaphore_signal(barrier, inc=1, device_id=partner, device_id_type=MESH)
 
     def load(slot):
-        d, h, c = uses[slot]
-        start = pl.multiple_of(block(d, h, c) * width, width)
+        start = pl.multiple_of(block(*uses[slot]) * width, width)
         return pltpu.make_async_copy(
             codes.at[:, pl.ds(start, width)], held.at[slot], load_sem.at[slot]
         )
 
-    for h in range(HALVES):
-        atom_copy(h).start()
-    partners = [other] + [CORES * flip(chip, b) + core for b in bits]
-    barrier = pltpu.get_barrier_semaphore()
-    for partner in partners:
-        pl.semaphore_signal(barrier, inc=1, device_id={"blk": partner}, device_id_type=MESH)
     for slot in range(len(uses)):
         load(slot).start()
-
     target_copy = pltpu.make_async_copy(signals, target, target_sem)
     target_copy.start()
 
     sends = []
 
-    def net(d, h, b):
-        place = full.at[block(d, h, 0)]
+    def net(d, u, b):
+        place = full.at[block(d, u, 0)]
         copy = pltpu.make_async_remote_copy(
-            place, place, net_send.at[len(sends)], net_recv.at[(d ^ b) * HALVES + h],
+            place, place, net_send.at[len(sends)], net_recv.at[d ^ b, u],
             device_id={"blk": CORES * flip(chip, b) + core}, device_id_type=MESH,
         )
         copy.start()
         sends.append(copy)
 
-    def across(d, h, c):
-        place = full.at[block(d, h, c)]
-        index = d * HALVES + h
+    def pair(d, u):
+        place = full.at[block(d, u, 0)]
         return pltpu.make_async_remote_copy(
-            place, place, core_send.at[index], core_recv.at[index],
+            place, place, pair_send.at[d, u - lead[0]], net_recv.at[d, u + 2],
+            device_id={"narrow": z + 1 - 2 * odd}, device_id_type=MESH,
+        )
+
+    def across(d, u, c):
+        place = full.at[block(d, u, c)]
+        return pltpu.make_async_remote_copy(
+            place, place, core_send.at[d, u], core_recv.at[d, u],
             device_id={"blk": other}, device_id_type=MESH,
         )
 
-    def arrived(d, h):
-        place = full.at[block(d, h, 0)]
+    def arrived(d, u):
+        place = full.at[block(d, u, 0)]
         pltpu.make_async_remote_copy(
-            place, place, net_send.at[0], net_recv.at[d * HALVES + h],
+            place, place, net_send.at[0], net_recv.at[d, u],
             device_id={"blk": other}, device_id_type=MESH,
         ).wait_recv()
 
-    def use(d, h, c):
-        slot = uses.index((d, h, c))
+    def use(d, u, c):
+        slot = uses.index((d, u, c))
         load(slot).wait()
-        total[...] += nt_dot(held[slot], full[block(d, h, c)])
-
-    for h in range(HALVES):
-        atom_copy(h).wait()
+        total[...] += nt_dot(held[slot], full[block(d, u, c)])
+
+    def send_own(units):
+        for step in range(len(units)):
+            for i, b in enumerate(bits):
+                net(0, units[-1 - step] if i == 0 else units[step], b)
+
+    for copy in atom_copies:
+        copy.wait()
     pl.semaphore_wait(barrier, len(partners))
-    for step in range(HALVES):
-        for i, b in enumerate(bits):
-            h = 1 - step if i == 0 else step
-            net(0, h, b)
-        across(0, step, 0).start()
+    send_own(lead or rest)
+    for d, u in own:
+        across(d, u, 0).start()
     total[...] = jnp.zeros_like(total)
+    for d, u in own:
+        use(d, u, 0)
     waiting = []
-    for d, h in order:
-        if d:
-            arrived(d, h)
-            for b in children(d, h, bits):
-                net(d, h, b)
-            across(d, h, 0).start()
-        use(d, h, 0)
-        waiting.append((d, h))
-        if len(waiting) > 1:
-            e, k = waiting.pop(0)
-            across(e, k, 1).wait_recv()
-            use(e, k, 1)
-    for e, k in waiting:
-        across(e, k, 1).wait_recv()
-        use(e, k, 1)
+    relayed = 0
+    for d, u in order:
+        arrived(d, u)
+        for b in branches(d, u):
+            net(d, u, b)
+        if u in lead:
+            pair(d, u).start()
+        across(d, u, 0).start()
+        relayed += 1
+        if lead and relayed == min(len(bits), len(order)):
+            send_own(rest)
+        if relayed == len(bits):
+            for e, v in own:
+                across(e, v, 1).wait_recv()
+                use(e, v, 1)
+        use(d, u, 0)
+        waiting.append((d, u))
+        if len(waiting) > 2:
+            e, v = waiting.pop(0)
+            across(e, v, 1).wait_recv()
+            use(e, v, 1)
+    for e, v in waiting:
+        across(e, v, 1).wait_recv()
+        use(e, v, 1)
     target_copy.wait()
     rounded = (total[...] - target[...].astype(jnp.float32)).astype(jnp.bfloat16)
     misfit[...] = (rounded.astype(jnp.float32) * -4.0).astype(jnp.bfloat16)
     for copy in sends:
         copy.wait_send()
-    for d, h in order:
-        across(d, h, 0).wait_send()
+    for d, u in own + order:
+        across(d, u, 0).wait_send()
+        if d and u in lead:
+            pair(d, u).wait_send()
 
 
 def update_kernel(together, codes, signals, full, misfit, fresh, made, misfit_two, total, store_sem):
@@ -209,7 +246,7 @@
     bits = bits_of(chips)
     return [
         (d, b) for d in range(chips) for b in bits
-        if any(b in children(d, t, bits) for t in range(HALVES))
+        if any(b in children(d, t, bits) for t in range(TREES))
     ]
 
 
@@ -238,7 +275,7 @@
 
     def term(d, h, c):
         owner = CORES * flip(chip, d) + (core if c == 0 else 1 - core)
-        return jnp.dot(misfit[...], made[owner * HALVES + h], preferred_element_type=jnp.float32)
+        return jnp.dot(misfit[...], made[owner * UNITS + h], preferred_element_type=jnp.float32)
 
     def span(k):
         start = slices[k][0][0]
@@ -252,7 +289,7 @@
         )
 
     def compute(into, d, c):
-        for h in range(HALVES):
+        for h in range(UNITS):
             into[d, :, h * width:(h + 1) * width] = term(d, h, c).astype(into.dtype)
 
     def net(d, k, t):
@@ -285,12 +322,12 @@
         net_out[d - 1, start:start + size] = summed(d, k, t).astype(jnp.bfloat16)
         net(d, k, t).start()
 
-    away = sorted(((d, t) for d in range(1, chips) for t in range(HALVES)), key=lambda p: -ones(p[0]))
+    away = sorted(((d, t) for d in range(1, chips) for t in range(TREES)), key=lambda p: -ones(p[0]))
     firsts = [p for p in away if not children(*p, bits)]
     relays = [p for p in away if children(*p, bits)]
 
     def arrive(k):
-        for t in range(HALVES):
+        for t in range(TREES):
             start, size = slices[k][t]
             value = summed(0, k, t)
             for j in range(line):
@@ -369,9 +406,8 @@
     rows, count = codes.shape
     atoms, features = dictionary.shape
     chips = blk // CORES
-    width = atoms // HALVES
-    blocks = blk * HALVES
-    pieces = chips * HALVES
+    width = atoms // UNITS
+    blocks = blk * UNITS
     part = atoms // line
     bf16, f32 = jnp.bfloat16, jnp.float32
     hbm_spec = pl.BlockSpec(memory_space=pltpu.HBM)
@@ -380,7 +416,7 @@
     size = 2 * rows * count
 
     full, misfit = pl.pallas_call(
-        functools.partial(gather_kernel, chips),
+        functools.partial(gather_kernel, chips, line),
         out_shape=(
             jax.ShapeDtypeStruct((blocks, features, width), bf16),
             jax.ShapeDtypeStruct((rows, features), bf16),
@@ -391,9 +427,9 @@
             VMEM((blocks, rows, width), bf16),
             VMEM((rows, features), bf16),
             VMEM((rows, features), f32),
-            DMA((blocks,)), DMA, DMA((HALVES,)),
-            DMA((HALVES * max(chips - 1, 1),)), DMA((pieces,)),
-            DMA((pieces,)), DMA((pieces,)),
+            DMA((blocks,)), DMA, DMA((UNITS,)),
+            DMA((UNITS * max(chips - 1, 1),)), DMA((chips, UNITS)), DMA((chips, TREES)),
+            DMA((chips, UNITS)), DMA((chips, UNITS)),
         ],
         compiler_params=pltpu.CompilerParams(
             collective_id=0, has_side_effects=True, vmem_limit_bytes=32 * 2**20
@@ -403,7 +439,7 @@
     )(in_hbm(codes), in_hbm(signals), in_hbm(dictionary.T))
 
     fresh, made, misfit_two = pl.pallas_call(
-        functools.partial(update_kernel, 4),
+        functools.partial(update_kernel, 2 * UNITS),
         out_shape=(
             jax.ShapeDtypeStruct((rows, count), bf16),
             jax.ShapeDtypeStruct((blocks, rows, width), bf16),
@@ -438,7 +474,7 @@
             VMEM((max(line - 1, 1), features, part), bf16),
             VMEM((max(line - 1, 1), features, part), bf16),
             DMA((chips, count_of)), DMA((chips, count_of)),
-            DMA((far, count_of, HALVES)), DMA((gaps, count_of, HALVES)),
+            DMA((far, count_of, TREES)), DMA((gaps, count_of, TREES)),
             DMA((max(line - 1, 1), count_of)), DMA((max(line - 1, 1), count_of)),
         ],
         compiler_params=pltpu.CompilerParams(

time: 65.3 us -> 64.2 us (0.983)
  Pallas kernels: 63.8 us -> 62.7 us
    pallas_call x2, Pallas kernels: 30.3 us -> 29.1 us  [the longest x1 24.3 us: body(): pl.pallas_call(functools.partial(gather_kernel, chips, line), out_shape=(...]
where the time goes in v6:
time: 64.2 us; the launch traced here: 64.1 us
  Pallas kernels  62.7 us (98%)
  local copies, waits for them, and re-layouts  0.72 us (1%)
  between operations  0.69 us (1%)
    pallas_call x1, Pallas kernels, body(): pl.pallas_call(functools.partial(gradient_kernel, chips, line, float(rows...  33.6 us
    pallas_call x1, Pallas kernels, body(): pl.pallas_call(functools.partial(gather_kernel, chips, line), out_shape=(...  24.3 us
    pallas_call x1, Pallas kernels, body(): pl.pallas_call(functools.partial(update_kernel, 2 * UNITS), out_shape=(ja...  4.8 us

profile of v6, /device:TPU:0, one launch (start us, length us, event | category | flops | bytes accessed | tf_op | source)
XLA Modules:
  0.0 64.1 jit_solution(17920187342123747290)
XLA Ops:
  0.6 0.0 copy-start.1
  0.6 0.0 copy-start
  0.6 24.3 %gather_atoms.1 = (bf16[48,192,256]{2,1,0:T(8,128)(2,1)S(1)}, bf16[192,192]{1,0:T(8,128)(2,1)S(1)}) custom-call(bf16[192,12288]{1,0:T(8,128)(2,1)} %codes.3, bf16[192,192]{1,0:T(8,128)(2,1)} %signals.3, bf16[192,1536]{1,0:T(8,128)(2,1)} %bitcast.3), custom_call_target="tpu_custom_call" | custom-call | flops 905969664 | bytes 9437184 | tf_op jit(solution)/shard_map/gather_atoms/pallas_call | solution.py:418
  25.0 0.0 copy-done.1
  25.0 0.0 copy-done
  25.0 4.8 %update_codes.1 = (bf16[192,12288]{1,0:T(8,128)(2,1)}, bf16[48,192,256]{2,1,0:T(8,128)(2,1)S(1)}, bf16[192,192]{1,0:T(8,128)(2,1)S(1)}) custom-call(bf16[192,12288]{1,0:T(8,128)(2,1)S(1)} %copy-done, bf16[192,192]{1,0:T(8,128)(2,1)S(1)} %copy-done.1, bf16[48,192,256]{2,1,0:T(8,128)(2,1)S(1)} %get-tuple-element.7.full, ...), custom_call_target="tpu_custom_call" | custom-call | flops 1811939328 | bytes 14155776 | tf_op jit(solution)/shard_map/update_codes/pallas_call | solution.py:441
  29.8 33.6 %dictionary_gradient.1 = f32[192,384]{1,0:T(8,128)S(1)} custom-call(bf16[48,192,256]{2,1,0:T(8,128)(2,1)S(1)} %get-tuple-element.10.made, bf16[192,192]{1,0:T(8,128)(2,1)S(1)} %get-tuple-element.11.misfit), custom_call_target="tpu_custom_call" | custom-call | flops 905969664 | bytes 9437184 | tf_op jit(solution)/shard_map/dictionary_gradient/pallas_call | solution.py:462
  63.4 0.7 %copy.6 = f32[384,192]{0,1:T(8,128)} copy(f32[384,192]{0,1:T(8,128)S(1)} %bitcast.2) | data formatting | bytes 589824
Async XLA Ops:
  0.6 24.3 %copy-start.1 = (bf16[192,192]{1,0:T(8,128)(2,1)S(1)}, bf16[192,192]{1,0:T(8,128)(2,1)}, u32[]{:S(2)}) copy-start(bf16[192,192]{1,0:T(8,128)(2,1)} %signals.3) | copy-start | bytes 221188
  0.6 24.3 %copy-start = (bf16[192,12288]{1,0:T(8,128)(2,1)S(1)}, bf16[192,12288]{1,0:T(8,128)(2,1)}, u32[]{:S(2)}) copy-start(bf16[192,12288]{1,0:T(8,128)(2,1)} %codes.3) | copy-start | bytes 14155780

commit v7 on v6

--- a/solution.py
+++ b/solution.py
@@ -179,7 +179,7 @@
         relayed += 1
         if lead and relayed == min(len(bits), len(order)):
             send_own(rest)
-        if relayed == len(bits):
+        if relayed == max(len(sort(lead, range(chips))), 1):
             for e, v in own:
                 across(e, v, 1).wait_recv()
                 use(e, v, 1)
@@ -223,9 +223,11 @@
             moved = codes[:, pl.ds(start, width)].astype(jnp.float32) + change
             made[i] = (moved - jnp.clip(moved, -0.5, 0.5)).astype(jnp.bfloat16)
             store(i).start()
+        value = total[...]
         for j in range(together):
             i = step * together + j
-            total[...] += nt_dot(made[i], full[i])
+            value += nt_dot(made[i], full[i])
+        total[...] = value
 
     left = total[...] - signals[...].astype(jnp.float32)
     misfit_two[...] = left.T.astype(jnp.bfloat16)
@@ -234,12 +236,8 @@
 
 
 def slices_of(features):
-    unit = features // 12
-    ranges, start = [], 0
-    for size in (unit, 2 * unit, 2 * unit, unit):
-        ranges.append([(start, size), (start + size, size)])
-        start += 2 * size
-    return ranges
+    size = features // 12
+    return [[(start, size), (start + size, size)] for start in range(0, features, 2 * size)]
 
 
 def gaps_of(chips):

time: 64.2 us -> 69 us (1.075)
  Pallas kernels: 62.7 us -> 67.4 us
    pallas_call x1, Pallas kernels: 33.6 us -> 38.5 us  [body(): pl.pallas_call(functools.partial(gradient_kernel, chips, line, float(rows...]
where the time goes in v7:
time: 69 us; the launch traced here: 68.8 us
  Pallas kernels  67.4 us (98%)
  local copies, waits for them, and re-layouts  0.72 us (1%)
    pallas_call x1, Pallas kernels, body(): pl.pallas_call(functools.partial(gradient_kernel, chips, line, float(rows...  38.5 us
    pallas_call x1, Pallas kernels, body(): pl.pallas_call(functools.partial(gather_kernel, chips, line), out_shape=(...  24.3 us
    pallas_call x1, Pallas kernels, body(): pl.pallas_call(functools.partial(update_kernel, 2 * UNITS), out_shape=(ja...  4.62 us

profile of v7, /device:TPU:0, one launch (start us, length us, event | category | flops | bytes accessed | tf_op | source)
XLA Modules:
  0.0 68.8 jit_solution(9507240661667532434)
XLA Ops:
  0.6 0.0 copy-start.1
  0.6 0.0 copy-start
  0.6 24.3 %gather_atoms.1 = (bf16[48,192,256]{2,1,0:T(8,128)(2,1)S(1)}, bf16[192,192]{1,0:T(8,128)(2,1)S(1)}) custom-call(bf16[192,12288]{1,0:T(8,128)(2,1)} %codes.3, bf16[192,192]{1,0:T(8,128)(2,1)} %signals.3, bf16[192,1536]{1,0:T(8,128)(2,1)} %bitcast.3), custom_call_target="tpu_custom_call" | custom-call | flops 905969664 | bytes 9437184 | tf_op jit(solution)/shard_map/gather_atoms/pallas_call | solution.py:416
  25.0 0.0 copy-done.1
  25.0 0.0 copy-done
  25.0 4.6 %update_codes.1 = (bf16[192,12288]{1,0:T(8,128)(2,1)}, bf16[48,192,256]{2,1,0:T(8,128)(2,1)S(1)}, bf16[192,192]{1,0:T(8,128)(2,1)S(1)}) custom-call(bf16[192,12288]{1,0:T(8,128)(2,1)S(1)} %copy-done, bf16[192,192]{1,0:T(8,128)(2,1)S(1)} %copy-done.1, bf16[48,192,256]{2,1,0:T(8,128)(2,1)S(1)} %get-tuple-element.7.full, ...), custom_call_target="tpu_custom_call" | custom-call | flops 1811939328 | bytes 14155776 | tf_op jit(solution)/shard_map/update_codes/pallas_call | solution.py:439
  29.6 38.5 %dictionary_gradient.1 = f32[192,384]{1,0:T(8,128)S(1)} custom-call(bf16[48,192,256]{2,1,0:T(8,128)(2,1)S(1)} %get-tuple-element.10.made, bf16[192,192]{1,0:T(8,128)(2,1)S(1)} %get-tuple-element.11.misfit), custom_call_target="tpu_custom_call" | custom-call | flops 905969664 | bytes 9437184 | tf_op jit(solution)/shard_map/dictionary_gradient/pallas_call | solution.py:460
  68.1 0.7 %copy.6 = f32[384,192]{0,1:T(8,128)} copy(f32[384,192]{0,1:T(8,128)S(1)} %bitcast.2) | data formatting | bytes 589824
Async XLA Ops:
  0.6 24.3 %copy-start.1 = (bf16[192,192]{1,0:T(8,128)(2,1)S(1)}, bf16[192,192]{1,0:T(8,128)(2,1)}, u32[]{:S(2)}) copy-start(bf16[192,192]{1,0:T(8,128)(2,1)} %signals.3) | copy-start | bytes 221188
  0.6 24.3 %copy-start = (bf16[192,12288]{1,0:T(8,128)(2,1)S(1)}, bf16[192,12288]{1,0:T(8,128)(2,1)}, u32[]{:S(2)}) copy-start(bf16[192,12288]{1,0:T(8,128)(2,1)} %codes.3) | copy-start | bytes 14155780

commit v8 on v7

--- a/solution.py
+++ b/solution.py
@@ -236,7 +236,7 @@
 
 
 def slices_of(features):
-    size = features // 12
+    size = features // 6
     return [[(start, size), (start + size, size)] for start in range(0, features, 2 * size)]
 
 

time: 69 us -> 63.1 us (0.914)
  Pallas kernels: 67.4 us -> 61.5 us
    pallas_call x1, Pallas kernels: 38.5 us -> 32.6 us  [body(): pl.pallas_call(functools.partial(gradient_kernel, chips, line, float(rows...]
where the time goes in v8:
time: 63.1 us; the launch traced here: 63 us
  Pallas kernels  61.5 us (97%)
  local copies, waits for them, and re-layouts  0.72 us (1%)
  between operations  0.69 us (1%)
    pallas_call x1, Pallas kernels, body(): pl.pallas_call(functools.partial(gradient_kernel, chips, line, float(rows...  32.6 us
    pallas_call x1, Pallas kernels, body(): pl.pallas_call(functools.partial(gather_kernel, chips, line), out_shape=(...  24.3 us
    pallas_call x1, Pallas kernels, body(): pl.pallas_call(functools.partial(update_kernel, 2 * UNITS), out_shape=(ja...  4.62 us

profile of v8, /device:TPU:0, one launch (start us, length us, event | category | flops | bytes accessed | tf_op | source)
XLA Modules:
  0.0 63.0 jit_solution(11729423503998255054)
XLA Ops:
  0.6 0.0 copy-start.1
  0.6 0.0 copy-start
  0.6 24.3 %gather_atoms.1 = (bf16[48,192,256]{2,1,0:T(8,128)(2,1)S(1)}, bf16[192,192]{1,0:T(8,128)(2,1)S(1)}) custom-call(bf16[192,12288]{1,0:T(8,128)(2,1)} %codes.3, bf16[192,192]{1,0:T(8,128)(2,1)} %signals.3, bf16[192,1536]{1,0:T(8,128)(2,1)} %bitcast.3), custom_call_target="tpu_custom_call" | custom-call | flops 905969664 | bytes 9437184 | tf_op jit(solution)/shard_map/gather_atoms/pallas_call | solution.py:416
  25.0 0.0 copy-done.1
  25.0 0.0 copy-done
  25.0 4.6 %update_codes.1 = (bf16[192,12288]{1,0:T(8,128)(2,1)}, bf16[48,192,256]{2,1,0:T(8,128)(2,1)S(1)}, bf16[192,192]{1,0:T(8,128)(2,1)S(1)}) custom-call(bf16[192,12288]{1,0:T(8,128)(2,1)S(1)} %copy-done, bf16[192,192]{1,0:T(8,128)(2,1)S(1)} %copy-done.1, bf16[48,192,256]{2,1,0:T(8,128)(2,1)S(1)} %get-tuple-element.7.full, ...), custom_call_target="tpu_custom_call" | custom-call | flops 1811939328 | bytes 14155776 | tf_op jit(solution)/shard_map/update_codes/pallas_call | solution.py:439
  29.6 32.6 %dictionary_gradient.1 = f32[192,384]{1,0:T(8,128)S(1)} custom-call(bf16[48,192,256]{2,1,0:T(8,128)(2,1)S(1)} %get-tuple-element.10.made, bf16[192,192]{1,0:T(8,128)(2,1)S(1)} %get-tuple-element.11.misfit), custom_call_target="tpu_custom_call" | custom-call | flops 905969664 | bytes 9437184 | tf_op jit(solution)/shard_map/dictionary_gradient/pallas_call | solution.py:460
  62.2 0.7 %copy.6 = f32[384,192]{0,1:T(8,128)} copy(f32[384,192]{0,1:T(8,128)S(1)} %bitcast.2) | data formatting | bytes 589824
Async XLA Ops:
  0.6 24.3 %copy-start.1 = (bf16[192,192]{1,0:T(8,128)(2,1)S(1)}, bf16[192,192]{1,0:T(8,128)(2,1)}, u32[]{:S(2)}) copy-start(bf16[192,192]{1,0:T(8,128)(2,1)} %signals.3) | copy-start | bytes 221188
  0.6 24.3 %copy-start = (bf16[192,12288]{1,0:T(8,128)(2,1)S(1)}, bf16[192,12288]{1,0:T(8,128)(2,1)}, u32[]{:S(2)}) copy-start(bf16[192,12288]{1,0:T(8,128)(2,1)} %codes.3) | copy-start | bytes 14155780

commit v9 on v8

--- a/solution.py
+++ b/solution.py
@@ -236,8 +236,12 @@
 
 
 def slices_of(features):
-    size = features // 6
-    return [[(start, size), (start + size, size)] for start in range(0, features, 2 * size)]
+    unit = features // 12
+    ranges, start = [], 0
+    for size in (2 * unit, 3 * unit, unit):
+        ranges.append([(start, size), (start + size, size)])
+        start += 2 * size
+    return ranges
 
 
 def gaps_of(chips):

time: 63.1 us -> 65 us (1.030)
  Pallas kernels: 61.5 us -> 63.4 us
    pallas_call x1, Pallas kernels: 32.6 us -> 34.5 us  [body(): pl.pallas_call(functools.partial(gradient_kernel, chips, line, float(rows...]
where the time goes in v9:
time: 65 us; the launch traced here: 64.8 us
  Pallas kernels  63.4 us (98%)
  local copies, waits for them, and re-layouts  0.72 us (1%)
  between operations  0.69 us (1%)
    pallas_call x1, Pallas kernels, body(): pl.pallas_call(functools.partial(gradient_kernel, chips, line, float(rows...  34.5 us
    pallas_call x1, Pallas kernels, body(): pl.pallas_call(functools.partial(gather_kernel, chips, line), out_shape=(...  24.3 us
    pallas_call x1, Pallas kernels, body(): pl.pallas_call(functools.partial(update_kernel, 2 * UNITS), out_shape=(ja...  4.62 us

profile of v9, /device:TPU:0, one launch (start us, length us, event | category | flops | bytes accessed | tf_op | source)
XLA Modules:
  0.0 64.8 jit_solution(16485201321186038994)
XLA Ops:
  0.6 0.0 copy-start.1
  0.6 0.0 copy-start
  0.6 24.3 %gather_atoms.1 = (bf16[48,192,256]{2,1,0:T(8,128)(2,1)S(1)}, bf16[192,192]{1,0:T(8,128)(2,1)S(1)}) custom-call(bf16[192,12288]{1,0:T(8,128)(2,1)} %codes.3, bf16[192,192]{1,0:T(8,128)(2,1)} %signals.3, bf16[192,1536]{1,0:T(8,128)(2,1)} %bitcast.3), custom_call_target="tpu_custom_call" | custom-call | flops 905969664 | bytes 9437184 | tf_op jit(solution)/shard_map/gather_atoms/pallas_call | solution.py:420
  25.0 0.0 copy-done.1
  25.0 0.0 copy-done
  25.0 4.6 %update_codes.1 = (bf16[192,12288]{1,0:T(8,128)(2,1)}, bf16[48,192,256]{2,1,0:T(8,128)(2,1)S(1)}, bf16[192,192]{1,0:T(8,128)(2,1)S(1)}) custom-call(bf16[192,12288]{1,0:T(8,128)(2,1)S(1)} %copy-done, bf16[192,192]{1,0:T(8,128)(2,1)S(1)} %copy-done.1, bf16[48,192,256]{2,1,0:T(8,128)(2,1)S(1)} %get-tuple-element.7.full, ...), custom_call_target="tpu_custom_call" | custom-call | flops 1811939328 | bytes 14155776 | tf_op jit(solution)/shard_map/update_codes/pallas_call | solution.py:443
  29.6 34.5 %dictionary_gradient.1 = f32[192,384]{1,0:T(8,128)S(1)} custom-call(bf16[48,192,256]{2,1,0:T(8,128)(2,1)S(1)} %get-tuple-element.10.made, bf16[192,192]{1,0:T(8,128)(2,1)S(1)} %get-tuple-element.11.misfit), custom_call_target="tpu_custom_call" | custom-call | flops 905969664 | bytes 9437184 | tf_op jit(solution)/shard_map/dictionary_gradient/pallas_call | solution.py:464
  64.1 0.7 %copy.6 = f32[384,192]{0,1:T(8,128)} copy(f32[384,192]{0,1:T(8,128)S(1)} %bitcast.2) | data formatting | bytes 589824
Async XLA Ops:
  0.6 24.3 %copy-start.1 = (bf16[192,192]{1,0:T(8,128)(2,1)S(1)}, bf16[192,192]{1,0:T(8,128)(2,1)}, u32[]{:S(2)}) copy-start(bf16[192,192]{1,0:T(8,128)(2,1)} %signals.3) | copy-start | bytes 221188
  0.6 24.3 %copy-start = (bf16[192,12288]{1,0:T(8,128)(2,1)S(1)}, bf16[192,12288]{1,0:T(8,128)(2,1)}, u32[]{:S(2)}) copy-start(bf16[192,12288]{1,0:T(8,128)(2,1)} %codes.3) | copy-start | bytes 14155780
